TPU v7x, 256 devices: a whole 4x4x8 slice. The times are simulated.
256 devices in a mesh: lon: 64 (over x, z, y_lo), lat: 4 (over y_hi, core).
Axes of the slice: x: 4, y: 4 (y_hi: 2, y_lo: 2; y = y_hi * 2 + y_lo), z: 8, core: 2. Of those that a mesh axis runs over, the one named last changes fastest.
Arguments:
- wind: float32 [2, 24, 64, 8192], P(None, None, 'lat', 'lon'), may hold values from -3 to 6
- tracers: float32 [4, 24, 64, 8192], P(None, None, 'lat', 'lon'), may hold values from -6 to 6
- cell_off: int32 [2, 24, 64, 8192], P(None, None, 'lat', 'lon'), may hold values from -2 to 6, as said below
Outputs:
- advected: float32 [6, 24, 64, 8192], P(None, None, 'lat', 'lon')
Inputs may be any that keep to these rules, and one draw needn't show every extreme that they name: `cell_off`: column offsets lie in -2 to 6 and row offsets in -2 to 2; both ends of each are taken in every draw.
All inputs are finite; a program needn't handle non-finite values.
Results may differ from a plain program's by a relative error of at most 0.0003.
Values sent between devices are 32-bit elements; how exact they have to be, the bound alone decides.
No kernel may reach another device: no remote copies, remote signals or barrier semaphores. Data moves between devices by JAX's collectives and lax.ppermute only.
A program may use at most 128 MiB of HBM per device.

v0:
```python
import jax
import jax.numpy as jnp
from jax import lax
from jax.sharding import PartitionSpec as P

MAXOFF = 6


def padded_2(cells, sides, width):
    for axis, dim in sides:
        count = lax.axis_size(axis)
        head = lax.slice_in_dim(cells, 0, width, axis=dim)
        tail = lax.slice_in_dim(cells, cells.shape[dim] - width, cells.shape[dim], axis=dim)
        cells = jnp.concatenate(
            [
                lax.ppermute(tail, axis, [(i, (i + 1) % count) for i in range(count)]),
                cells,
                lax.ppermute(head, axis, [((i + 1) % count, i) for i in range(count)]),
            ],
            axis=dim,
        )
    return cells


def cubic_weights(frac):
    return (
        -frac * (frac - 1.0) * (frac - 2.0) / 6.0,
        (frac + 1.0) * (frac - 1.0) * (frac - 2.0) / 2.0,
        -(frac + 1.0) * frac * (frac - 2.0) / 2.0,
        (frac + 1.0) * frac * (frac - 1.0) / 6.0,
    )


def spread_taps(offset, taps, lowest, count):
    spread = []
    for slot in range(count):
        target = lowest + slot
        total = None
        for added, weight in taps:
            term = jnp.where(added - offset == target, weight, 0.0)
            total = term if total is None else total + term
        spread.append(total)
    return spread


def shifted_sum(
    padded, col_weights, col_low, row_weights, row_low, row_margin, col_margin, height, breadth
):
    total = None
    for row_slot, row_weight in enumerate(row_weights):
        row_start = row_margin + row_low + row_slot
        inner = None
        for col_slot, col_weight in enumerate(col_weights):
            col_start = col_margin + col_low + col_slot
            piece = padded[:, :, row_start : row_start + height, col_start : col_start + breadth]
            term = col_weight * piece
            inner = term if inner is None else inner + term
        outer = row_weight * inner
        total = outer if total is None else total + outer
    return total


def advect(wind_pad, tracer_pad, wind, col_off, row_off, row_margin, col_margin):
    height = wind.shape[2]
    breadth = wind.shape[3]
    col_float = col_off.astype(jnp.float32)
    row_float = row_off.astype(jnp.float32)
    disp_east = wind[0]
    disp_north = wind[1]
    for repeat in range(2):
        frac_x = jnp.clip(col_float - disp_east, 0.0, 1.0)
        frac_y = jnp.clip(row_float - disp_north, 0.0, 1.0)
        col_weights = spread_taps(col_off, ((0, 1.0 - frac_x), (1, frac_x)), -MAXOFF, MAXOFF + 4)
        row_weights = spread_taps(row_off, ((0, 1.0 - frac_y), (1, frac_y)), -2, 6)
        depart = shifted_sum(
            wind_pad, col_weights, -MAXOFF, row_weights, -2, row_margin, col_margin, height, breadth
        )
        disp_east = 0.5 * (wind[0] + depart[0])
        disp_north = 0.5 * (wind[1] + depart[1])
    frac_x = jnp.clip(col_float - disp_east, 0.0, 1.0)
    frac_y = jnp.clip(row_float - disp_north, 0.0, 1.0)
    weight_x = cubic_weights(frac_x)
    weight_y = cubic_weights(frac_y)
    col_taps = tuple(((step - 1, weight_x[step]) for step in range(4)))
    row_taps = tuple(((step - 1, weight_y[step]) for step in range(4)))
    col_weights = spread_taps(col_off, col_taps, -(MAXOFF + 1), MAXOFF + 6)
    row_weights = spread_taps(row_off, row_taps, -3, 8)
    results = []
    for padded in (wind_pad, tracer_pad):
        results.append(
            shifted_sum(
                padded,
                col_weights,
                -(MAXOFF + 1),
                row_weights,
                -3,
                row_margin,
                col_margin,
                height,
                breadth,
            )
        )
    return jnp.concatenate(results, axis=0)


def clear_bands(padded, margin_width):
    local_rows = padded.shape[2] - 2 * margin_width
    global_row = (
        lax.axis_index("lat") * local_rows
        + jnp.arange(padded.shape[2], dtype=jnp.int32)
        - margin_width
    )
    inside = (global_row >= 0) & (global_row < local_rows * lax.axis_size("lat"))
    return jnp.where(inside[:, None], padded, 0.0)


def extend_wind(fields):
    margin_width = max(MAXOFF + 1, 4)
    padded = padded_2(fields, (("lon", 3), ("lat", 2)), margin_width)
    return (clear_bands(padded, margin_width), margin_width, margin_width)


def extend_tracers(fields):
    margin_width = max(MAXOFF + 1, 4)
    padded = padded_2(fields, (("lon", 3), ("lat", 2)), margin_width)
    return clear_bands(padded, margin_width)


def shards(wind, tracers, cell_off):
    wind_pad, row_margin, col_margin = extend_wind(wind)
    tracer_pad = extend_tracers(tracers)
    return advect(wind_pad, tracer_pad, wind, cell_off[0], cell_off[1], row_margin, col_margin)


def solution(mesh):
    placed = (P(None, None, "lat", "lon"), P(None, None, "lat", "lon"), P(None, None, "lat", "lon"))
    return jax.shard_map(
        shards, mesh=mesh, in_specs=placed, out_specs=P(None, None, "lat", "lon"), check_vma=False
    )
```

profile of v0, /device:TPU:1, one launch (start us, length us, event | category | flops | bytes accessed | tf_op | source)
XLA Modules:
  0.0 112.7 jit_solution(7963045585967554546)
XLA Ops:
  0.0 1.6 %fusion.236 = (f32[4,24,16,7]{3,2,1,0:T(8,128)S(1)}, f32[4,24,16,7]{3,2,1,0:T(8,128)S(1)}) fusion(f32[4,24,16,128]{3,2,1,0:T(8,128)} %param.4), kind=kLoop, calls=%fused_computation.484 | loop fusion | bytes 172032 | tf_op jit(solution)/shard_map/slice | solution.py:13
  1.7 1.2 %copy.20 = f32[4,24,16,7]{1,2,3,0:T(8,128)} copy(f32[4,24,16,7]{3,2,1,0:T(8,128)S(1)} %get-tuple-element.55) | data formatting | bytes 86016
  2.9 9.6 %collective-permute-start.5 = (f32[4,24,16,7]{1,2,3,0:T(8,128)}, f32[4,24,16,7]{1,2,3,0:T(8,128)}, u32[]{:S(2)}, u32[]{:S(2)}) collective-permute-start(f32[4,24,16,7]{1,2,3,0:T(8,128)} %copy.20), channel_id=1, source_target_pairs={{4,0},{8,4},{12,8},{16,12},{20,16},{24,20},{28,24},{32,28},{36,32}... | collective-permute-start | bytes 129032 | tf_op jit(solution)/shard_map/ppermute | solution.py:18
  12.5 1.2 %copy.19 = f32[4,24,16,7]{1,2,3,0:T(8,128)} copy(f32[4,24,16,7]{3,2,1,0:T(8,128)S(1)} %get-tuple-element.54) | data formatting | bytes 86016
  13.7 0.1 copy.5
  13.9 0.2 fusion.238
  14.0 5.8 %collective-permute-start.1 = (f32[2,24,16,7]{3,1,2,0:T(8,128)S(1)}, f32[2,24,16,7]{3,1,2,0:T(8,128)S(1)}, u32[]{:S(2)}, u32[]{:S(2)}) collective-permute-start(f32[2,24,16,7]{3,1,2,0:T(8,128)S(1)} %get-tuple-element.113), channel_id=1, source_target_pairs={{4,0},{8,4},{12,8},{16,12},{20,16},{24,20},{28,24},{32,28},{36,32}... | collective-permute-start | bytes 64520 | tf_op jit(solution)/shard_map/ppermute | solution.py:18
  19.8 1.0 add_bitcast_fusion.50
  20.8 2.0 %add_bitcast_fusion.49 = (f32[24,16,128]{2,0,1:T(8,128)}, pred[1,24,16,128]{3,1,2,0:T(8,128)(4,1)}, pred[1,24,16,128]{3,1,2,0:T(8,128)(4,1)}, f32[24,16,128]{2,0...) fusion(f32[1,24,16,128]{3,1,2,0:T(8,128)S(1)} %get-tuple-elemen, ...), kind=kLoop, calls=%fused_computation.436 | loop fusion | flops 2359296 | bytes 3047424 | tf_op jit(solution)/shard_map/mul | solution.py:56
  22.8 1.1 %add_bitcast_fusion.40 = (f32[24,16,128]{2,0,1:T(8,128)}, f32[24,16,128]{2,0,1:T(8,128)}, f32[24,16,128]{2,0,1:T(8,128)}, f32[24,16,128]{2,0,1:T(8,128)}, f32[24,16,128]{2,0,1:T(8,128)}) fusion(f32[1,24,16,128]{3,1,2,0:T(8,128)S(1)} %get-tuple-element.104, s32[1,24,16,128]{3,2,1,0:T(8,128)S(1)} %get-tuple-element.106), kind=kLoop, calls=%fused_computation.427 | loop fusion | flops 1376256 | bytes 1376256 | tf_op jit(solution)/shard_map/mul | solution.py:58
  24.0 13.1 %collective-permute-done.1 = f32[2,24,16,7]{3,1,2,0:T(8,128)S(1)} collective-permute-done((f32[2,24,16,7]{3,1,2,0:T(8,128)S(1)}, f32[2,24,16,7]{3,1,2,0:T(8,128)S(1)}, u32[]{:S(2)}, u32[]{:S(2)}) %collective-permute-start.1) | collective-permute-done | bytes 21536 | tf_op jit(solution)/shard_map/ppermute | solution.py:18
  37.1 1.2 %pad_maximum_fusion.6 = (f32[2,24,7,142]{3,1,2,0:T(8,128)}, f32[2,24,7,142]{3,1,2,0:T(8,128)}) fusion(f32[2,24,16,7]{3,1,2,0:T(8,128)S(1)} %collective-permute-done.1, f32[2,24,16,128]{3,1,2,0:T(8,128)S(1)} %copy.5, f32[2,24,16,7]{3,1,2,0:T(8,128)S(1)} %collective-permute-done), kind=kLoop, calls=%fused_computation.348 | loop fusion | flops 190848 | bytes 817920 | tf_op jit(solution)/shard_map/slice | solution.py:13
  38.3 1.9 %collective-permute-start.3 = (f32[2,24,7,142]{3,1,2,0:T(8,128)}, f32[2,24,7,142]{3,1,2,0:T(8,128)}, u32[]{:S(2)}, u32[]{:S(2)}) collective-permute-start(f32[2,24,7,142]{3,1,2,0:T(8,128)} %get-tuple-element.49), channel_id=1, source_target_pairs={{1,0},{2,1},{3,2},{0,3},{5,4},{6,5},{7,6},{4,7},{9,8},{10,9},{11,1... | collective-permute-start | bytes 572552 | tf_op jit(solution)/shard_map/ppermute | solution.py:18
  40.2 2.5 %collective-permute-start.2 = (f32[2,24,7,142]{3,1,2,0:T(8,128)}, f32[2,24,7,142]{3,1,2,0:T(8,128)}, u32[]{:S(2)}, u32[]{:S(2)}) collective-permute-start(f32[2,24,7,142]{3,1,2,0:T(8,128)} %get-tuple-element.48), channel_id=1, source_target_pairs={{0,1},{1,2},{2,3},{3,0},{4,5},{5,6},{6,7},{7,4},{8,9},{9,10},{10,1... | collective-permute-start | bytes 572552 | tf_op jit(solution)/shard_map/ppermute | solution.py:16
  42.7 0.2 copy.14
  43.0 1.4 %copy.15 = f32[4,24,16,7]{3,1,2,0:T(8,128)S(1)} copy(f32[4,24,16,7]{1,2,3,0:T(8,128)} %collective-permute-done.5) | data formatting | bytes 86016 | tf_op jit(solution)/shard_map/ppermute | solution.py:18
  44.4 1.7 %copy.13 = f32[4,24,16,7]{3,1,2,0:T(8,128)S(1)} copy(f32[4,24,16,7]{1,2,3,0:T(8,128)} %collective-permute-done.4) | data formatting | bytes 86016 | tf_op jit(solution)/shard_map/ppermute | solution.py:16
  46.1 1.7 %pad_maximum_fusion.3 = (f32[4,24,7,142]{3,1,2,0:T(8,128)}, f32[4,24,7,142]{3,1,2,0:T(8,128)}) fusion(f32[4,24,16,7]{3,1,2,0:T(8,128)S(1)} %copy.15, f32[4,24,16,128]{3,1,2,0:T(8,128)S(1)} %copy.14, f32[4,24,16,7]{3,1,2,0:T(8,128)S(1)} %copy.13), kind=kLoop, calls=%fused_computation.204 | loop fusion | flops 381696 | bytes 1635840 | tf_op jit(solution)/shard_map/slice | solution.py:13
  47.8 3.5 %collective-permute-start.6 = (f32[4,24,7,142]{3,1,2,0:T(8,128)}, f32[4,24,7,142]{3,1,2,0:T(8,128)}, u32[]{:S(2)}, u32[]{:S(2)}) collective-permute-start(f32[4,24,7,142]{3,1,2,0:T(8,128)} %get-tuple-element.46), channel_id=1, source_target_pairs={{0,1},{1,2},{2,3},{3,0},{4,5},{5,6},{6,7},{7,4},{8,9},{9,10},{10,1... | collective-permute-start | bytes 1145096 | tf_op jit(solution)/shard_map/ppermute | solution.py:16
  51.3 1.5 %maximum_select_fusion.1 = f32[2,24,30,142]{3,1,2,0:T(8,128)S(1)} fusion(f32[2,24,7,142]{3,1,2,0:T(8,128)} %collective-permute-done.3, f32[2,24,16,7]{3,1,2,0:T(8,128)S(1)} %collective-permute-done.1, f32[2,24,16,128]{3,1,2,0:T(8,128)S(1)} %copy.5, f32[2,24,16,7]{3,1,2,0:T(8,128)S(1)} %copy-done.13, f32[2,24,7,142]{3,1,2,0:T(8,128)} %collective-permute-done.2, ...), kind=kLoop, calls=%fused_computation.1 | loop fusion | flops 1022400 | bytes 1635870 | tf_op jit(solution)/shard_map/jit(_where)/select_n | solution.py:114
  52.9 7.6 %multiply_add_fusion.1 = f32[2,24,16,128]{3,1,2,0:T(8,128)S(1)} fusion(f32[2,24,30,142]{3,1,2,0:T(8,128)S(1)} %maximum_select_fusion.1, f32[24,16,128]{2,0,1:T(8,128)} %get-tuple-element.111, f32[24,16,128]{2,0,1:T(8,128)} %get-tuple-element.110, f32[24,16,128]{2,0,1:T(8,128)} %get-tuple-element.108, f32[24,16,128]{2,0,1:T(8,128)} %get-tuple-element.109, ...), kind=kLoop, calls=%fused_computation.345 | loop fusion | flops 12288000 | bytes 27131904 | tf_op jit(solution)/shard_map/add | solution.py:59
  60.7 1.0 add_bitcast_fusion.34
  61.8 1.1 add_bitcast_fusion.24
  63.0 1.1 add_bitcast_fusion.33
  64.1 7.5 %multiply_add_fusion = f32[2,24,16,128]{3,1,2,0:T(8,128)S(1)} fusion(f32[2,24,30,142]{3,1,2,0:T(8,128)S(1)} %maximum_select_fusion.1, f32[24,16,128]{2,0,1:T(8,128)} %get-tuple-element.78, f32[24,16,128]{2,0,1:T(8,128)} %get-tuple-element.77, f32[24,16,128]{2,0,1:T(8,128)} %get-tuple-element.75, f32[24,16,128]{2,0,1:T(8,128)} %get-tuple-element.76, ...), kind=kLoop, calls=%fused_computation.344 | loop fusion | flops 12288000 | bytes 27131904 | tf_op jit(solution)/shard_map/add | solution.py:59
  71.8 1.3 %add_bitcast_fusion.18 = (f32[24,16,128]{2,0,1:T(8,128)}, f32[1,24,16,128]{3,1,2,0:T(8,128)S(1)}, f32[24,16,128]{2,0,1:T(8,128)}, f32[1,24,16,128]{3,1,2,0:T(8,128)S(1)}) fusion(s32[1,24,16,128]{3,2,1,0:T(8,128)S(1)} %get-tuple-element.105, f32[2,24,16,128]{3,1,2,0:T(8,128)S(1)} %multiply_add_fusion, f32[2,24,16,128]{3,1,2,0:T(8,128)S(1)} %copy.5, ...), kind=kLoop, calls=%fused_computation.403 | loop fusion | flops 3637248 | bytes 1966080 | tf_op jit(solution)/shard_map/mul | solution.py:56
  73.2 2.2 %add_bitcast_fusion.17 = (f32[24,16,128]{2,0,1:T(8,128)S(1)}, f32[24,16,128]{2,0,1:T(8,128)S(1)}, f32[24,16,128]{2,0,1:T(8,128)}, f32[24,16,128]{2,0,1:T(8,128)}...) fusion(pred[1,24,16,128]{3,1,2,0:T(8,128)(4,1)S(1)} %copy-done., ...), kind=kLoop, calls=%fused_computation.402 | loop fusion | flops 5111808 | bytes 2949120 | tf_op jit(solution)/shard_map/mul | solution.py:56
  75.4 2.4 %add_bitcast_fusion.6 = (f32[24,16,128]{2,0,1:T(8,128)}, f32[24,16,128]{2,0,1:T(8,128)}, f32[24,16,128]{2,0,1:T(8,128)}, f32[24,16,128]{2,0,1:T(8,128)}, f32[24,...) fusion(s32[1,24,16,128]{3,2,1,0:T(8,128)S(1)} %get-tuple-elemen, ...), kind=kLoop, calls=%fused_computation.391 | loop fusion | flops 6635520 | bytes 2752512 | tf_op jit(solution)/shard_map/mul | solution.py:58
  77.7 11.5 %fusion.105 = f32[2,24,16,128]{3,1,2,0:T(8,128)} fusion(f32[2,24,30,142]{3,1,2,0:T(8,128)S(1)} %maximum_select_fusion.1, f32[24,16,128]{2,0,1:T(8,128)} %get-tuple-element.73, f32[24,16,128]{2,0,1:T(8,128)} %get-tuple-element.72, f32[24,16,128]{2,0,1:T(8,128)} %get-tuple-element.71, f32[24,16,128]{2,0,1:T(8,128)} %get-tuple-element.70, ...), kind=kLoop, calls=%fused_computation.208 | loop fusion | flops 19562496 | bytes 42074112 | tf_op jit(solution)/shard_map/add | solution.py:59
  89.3 2.5 %maximum_select_fusion = f32[4,24,30,142]{3,1,2,0:T(8,128)S(1)} fusion(f32[4,24,7,142]{3,1,2,0:T(8,128)} %collective-permute-done.7, f32[4,24,16,7]{3,1,2,0:T(8,128)S(1)} %copy-done.2, f32[4,24,16,128]{3,1,2,0:T(8,128)S(1)} %copy.14, f32[4,24,16,7]{3,1,2,0:T(8,128)} %copy-done.3, f32[4,24,7,142]{3,1,2,0:T(8,128)} %collective-permute-done.6, ...), kind=kLoop, calls=%fused_computation | loop fusion | flops 2044800 | bytes 3271710 | tf_op jit(solution)/shard_map/jit(_where)/select_n | solution.py:114
  91.9 19.5 %fusion.2 = f32[4,24,16,128]{3,1,2,0:T(8,128)S(1)} fusion(f32[4,24,30,142]{3,1,2,0:T(8,128)S(1)} %maximum_select_fusion, f32[24,16,128]{2,0,1:T(8,128)} %get-tuple-element.73, f32[24,16,128]{2,0,1:T(8,128)} %get-tuple-element.72, f32[24,16,128]{2,0,1:T(8,128)} %get-tuple-element.71, f32[24,16,128]{2,0,1:T(8,128)} %get-tuple-element.70, ...), kind=kLoop, calls=%fused_computation.6 | loop fusion | flops 39124992 | bytes 80216064 | tf_op jit(solution)/shard_map/add | solution.py:59
  111.5 1.2 %copy.16 = f32[6,24,16,128]{3,2,1,0:T(8,128)} copy(f32[6,24,16,128]{3,1,2,0:T(8,128)S(1)} %pad_maximum_fusion) | data formatting | bytes 2359296 | tf_op jit(solution)/shard_map/concatenate | solution.py:103
  (133 shorter events, 0.4 us)
Async XLA Ops:
  1.6 12.1 %copy-start.58 = (f32[2,24,16,128]{3,2,1,0:T(8,128)S(1)}, f32[2,24,16,128]{3,2,1,0:T(8,128)}, u32[]{:S(2)}) copy-start(f32[2,24,16,128]{3,2,1,0:T(8,128)} %param.3) | copy-start | bytes 1179652
  2.9 40.1 %collective-permute-start.5 = (f32[4,24,16,7]{1,2,3,0:T(8,128)}, f32[4,24,16,7]{1,2,3,0:T(8,128)}, u32[]{:S(2)}, u32[]{:S(2)}) collective-permute-start(f32[4,24,16,7]{1,2,3,0:T(8,128)} %copy.20), channel_id=1, source_target_pairs={{4,0},{8,4},{12,8},{16,12},{20,16},{24,20},{28,24},{32,28},{36,32}... | collective-permute-start | bytes 129032 | tf_op jit(solution)/shard_map/ppermute | solution.py:18
  12.5 7.3 %copy-start.59 = (s32[2,24,16,128]{3,2,1,0:T(8,128)S(1)}, s32[2,24,16,128]{3,2,1,0:T(8,128)}, u32[]{:S(2)}) copy-start(s32[2,24,16,128]{3,2,1,0:T(8,128)} %param.5) | copy-start | bytes 1179652
  13.7 30.6 %collective-permute-start.4 = (f32[4,24,16,7]{1,2,3,0:T(8,128)}, f32[4,24,16,7]{1,2,3,0:T(8,128)}, u32[]{:S(2)}, u32[]{:S(2)}) collective-permute-start(f32[4,24,16,7]{1,2,3,0:T(8,128)} %copy.19), channel_id=1, source_target_pairs={{0,4},{4,8},{8,12},{12,16},{16,20},{20,24},{24,28},{28,32},{32,36}... | collective-permute-start | bytes 129032 | tf_op jit(solution)/shard_map/ppermute | solution.py:16
  14.0 23.1 %collective-permute-start.1 = (f32[2,24,16,7]{3,1,2,0:T(8,128)S(1)}, f32[2,24,16,7]{3,1,2,0:T(8,128)S(1)}, u32[]{:S(2)}, u32[]{:S(2)}) collective-permute-start(f32[2,24,16,7]{3,1,2,0:T(8,128)S(1)} %get-tuple-element.113), channel_id=1, source_target_pairs={{4,0},{8,4},{12,8},{16,12},{20,16},{24,20},{28,24},{32,28},{36,32}... | collective-permute-start | bytes 64520 | tf_op jit(solution)/shard_map/ppermute | solution.py:18
  19.8 17.3 %collective-permute-start = (f32[2,24,16,7]{3,1,2,0:T(8,128)S(1)}, f32[2,24,16,7]{3,1,2,0:T(8,128)S(1)}, u32[]{:S(2)}, u32[]{:S(2)}) collective-permute-start(f32[2,24,16,7]{3,1,2,0:T(8,128)S(1)} %get-tuple-element.112), channel_id=1, source_target_pairs={{0,4},{4,8},{8,12},{12,16},{16,20},{20,24},{24,28},{28,32},{32,36}... | collective-permute-start | bytes 64520 | tf_op jit(solution)/shard_map/ppermute | solution.py:16
  22.8 19.9 %copy-start = (f32[4,24,16,128]{3,2,1,0:T(8,128)S(1)}, f32[4,24,16,128]{3,2,1,0:T(8,128)}, u32[]{:S(2)}) copy-start(f32[4,24,16,128]{3,2,1,0:T(8,128)} %param.4) | copy-start | bytes 2359300
  37.1 5.6 %copy-start.12 = (f32[2,24,16,7]{3,1,2,0:T(8,128)}, f32[2,24,16,7]{3,1,2,0:T(8,128)S(1)}, u32[]{:S(2)}) copy-start(f32[2,24,16,7]{3,1,2,0:T(8,128)S(1)} %collective-permute-done) | copy-start | bytes 64516
  38.3 13.0 %collective-permute-start.3 = (f32[2,24,7,142]{3,1,2,0:T(8,128)}, f32[2,24,7,142]{3,1,2,0:T(8,128)}, u32[]{:S(2)}, u32[]{:S(2)}) collective-permute-start(f32[2,24,7,142]{3,1,2,0:T(8,128)} %get-tuple-element.49), channel_id=1, source_target_pairs={{1,0},{2,1},{3,2},{0,3},{5,4},{6,5},{7,6},{4,7},{9,8},{10,9},{11,1... | collective-permute-start | bytes 572552 | tf_op jit(solution)/shard_map/ppermute | solution.py:18
  40.2 11.1 %collective-permute-start.2 = (f32[2,24,7,142]{3,1,2,0:T(8,128)}, f32[2,24,7,142]{3,1,2,0:T(8,128)}, u32[]{:S(2)}, u32[]{:S(2)}) collective-permute-start(f32[2,24,7,142]{3,1,2,0:T(8,128)} %get-tuple-element.48), channel_id=1, source_target_pairs={{0,1},{1,2},{2,3},{3,0},{4,5},{5,6},{6,7},{7,4},{8,9},{9,10},{10,1... | collective-permute-start | bytes 572552 | tf_op jit(solution)/shard_map/ppermute | solution.py:16
  44.4 3.4 %copy-start.1 = (f32[4,24,16,7]{3,1,2,0:T(8,128)}, f32[4,24,16,7]{3,1,2,0:T(8,128)S(1)}, u32[]{:S(2)}) copy-start(f32[4,24,16,7]{3,1,2,0:T(8,128)S(1)} %copy.15) | copy-start | bytes 129028
  46.0 5.3 %copy-start.13 = (f32[2,24,16,7]{3,1,2,0:T(8,128)S(1)}, f32[2,24,16,7]{3,1,2,0:T(8,128)}, u32[]{:S(2)}) copy-start(f32[2,24,16,7]{3,1,2,0:T(8,128)} %copy-done.12) | copy-start | bytes 64516
  47.8 41.5 %collective-permute-start.7 = (f32[4,24,7,142]{3,1,2,0:T(8,128)}, f32[4,24,7,142]{3,1,2,0:T(8,128)}, u32[]{:S(2)}, u32[]{:S(2)}) collective-permute-start(f32[4,24,7,142]{3,1,2,0:T(8,128)} %get-tuple-element.47), channel_id=1, source_target_pairs={{1,0},{2,1},{3,2},{0,3},{5,4},{6,5},{7,6},{4,7},{9,8},{10,9},{11,1... | collective-permute-start | bytes 1145096 | tf_op jit(solution)/shard_map/ppermute | solution.py:18
  47.8 5.1 %copy-start.14 = (f32[24,16,128]{2,0,1:T(8,128)S(1)}, f32[24,16,128]{2,0,1:T(8,128)}, u32[]{:S(2)}) copy-start(f32[24,16,128]{2,0,1:T(8,128)} %get-tuple-element.15) | copy-start | bytes 589828
  47.8 5.1 %copy-start.15 = (f32[24,16,128]{2,0,1:T(8,128)S(1)}, f32[24,16,128]{2,0,1:T(8,128)}, u32[]{:S(2)}) copy-start(f32[24,16,128]{2,0,1:T(8,128)} %get-tuple-element.103) | copy-start | bytes 589828
  47.8 5.1 %copy-start.16 = (f32[24,16,128]{2,0,1:T(8,128)S(1)}, f32[24,16,128]{2,0,1:T(8,128)}, u32[]{:S(2)}) copy-start(f32[24,16,128]{2,0,1:T(8,128)} %get-tuple-element.19) | copy-start | bytes 589828
  47.8 5.1 %copy-start.17 = (f32[24,16,128]{2,0,1:T(8,128)S(1)}, f32[24,16,128]{2,0,1:T(8,128)}, u32[]{:S(2)}) copy-start(f32[24,16,128]{2,0,1:T(8,128)} %get-tuple-element.79) | copy-start | bytes 589828
  47.8 5.1 %copy-start.18 = (f32[24,16,128]{2,0,1:T(8,128)S(1)}, f32[24,16,128]{2,0,1:T(8,128)}, u32[]{:S(2)}) copy-start(f32[24,16,128]{2,0,1:T(8,128)} %get-tuple-element.82) | copy-start | bytes 589828
  47.8 5.1 %copy-start.19 = (f32[24,16,128]{2,0,1:T(8,128)S(1)}, f32[24,16,128]{2,0,1:T(8,128)}, u32[]{:S(2)}) copy-start(f32[24,16,128]{2,0,1:T(8,128)} %get-tuple-element.85) | copy-start | bytes 589828
  47.8 41.5 %collective-permute-start.6 = (f32[4,24,7,142]{3,1,2,0:T(8,128)}, f32[4,24,7,142]{3,1,2,0:T(8,128)}, u32[]{:S(2)}, u32[]{:S(2)}) collective-permute-start(f32[4,24,7,142]{3,1,2,0:T(8,128)} %get-tuple-element.46), channel_id=1, source_target_pairs={{0,1},{1,2},{2,3},{3,0},{4,5},{5,6},{6,7},{7,4},{8,9},{9,10},{10,1... | collective-permute-start | bytes 1145096 | tf_op jit(solution)/shard_map/ppermute | solution.py:16
  52.9 7.6 %copy-start.20 = (pred[1,24,16,128]{3,1,2,0:T(8,128)(4,1)S(1)}, pred[1,24,16,128]{3,1,2,0:T(8,128)(4,1)}, u32[]{:S(2)}) copy-start(pred[1,24,16,128]{3,1,2,0:T(8,128)(4,1)} %get-tuple-element.16) | copy-start | bytes 147460
  52.9 7.6 %copy-start.21 = (pred[1,24,16,128]{3,1,2,0:T(8,128)(4,1)S(1)}, pred[1,24,16,128]{3,1,2,0:T(8,128)(4,1)}, u32[]{:S(2)}) copy-start(pred[1,24,16,128]{3,1,2,0:T(8,128)(4,1)} %get-tuple-element.17) | copy-start | bytes 147460
  60.5 2.3 %copy-start.22 = (pred[1,24,16,128]{3,1,2,0:T(8,128)(4,1)S(1)}, pred[1,24,16,128]{3,1,2,0:T(8,128)(4,1)}, u32[]{:S(2)}) copy-start(pred[1,24,16,128]{3,1,2,0:T(8,128)(4,1)} %get-tuple-element.20) | copy-start | bytes 147460
  77.7 11.6 %copy-start.2 = (f32[4,24,16,7]{3,1,2,0:T(8,128)S(1)}, f32[4,24,16,7]{3,1,2,0:T(8,128)}, u32[]{:S(2)}) copy-start(f32[4,24,16,7]{3,1,2,0:T(8,128)} %copy-done.1) | copy-start | bytes 129028
  89.2 2.6 %copy-start.4 = (f32[24,16,128]{2,0,1:T(8,128)S(1)}, f32[24,16,128]{2,0,1:T(8,128)}, u32[]{:S(2)}) copy-start(f32[24,16,128]{2,0,1:T(8,128)} %get-tuple-element.58) | copy-start | bytes 589828
  89.2 2.6 %copy-start.5 = (f32[24,16,128]{2,0,1:T(8,128)S(1)}, f32[24,16,128]{2,0,1:T(8,128)}, u32[]{:S(2)}) copy-start(f32[24,16,128]{2,0,1:T(8,128)} %get-tuple-element.59) | copy-start | bytes 589828
  89.2 2.6 %copy-start.6 = (f32[24,16,128]{2,0,1:T(8,128)S(1)}, f32[24,16,128]{2,0,1:T(8,128)}, u32[]{:S(2)}) copy-start(f32[24,16,128]{2,0,1:T(8,128)} %get-tuple-element.60) | copy-start | bytes 589828
  89.2 2.6 %copy-start.7 = (f32[24,16,128]{2,0,1:T(8,128)S(1)}, f32[24,16,128]{2,0,1:T(8,128)}, u32[]{:S(2)}) copy-start(f32[24,16,128]{2,0,1:T(8,128)} %get-tuple-element.61) | copy-start | bytes 589828
  89.3 2.6 %copy-start.8 = (f32[24,16,128]{2,0,1:T(8,128)S(1)}, f32[24,16,128]{2,0,1:T(8,128)}, u32[]{:S(2)}) copy-start(f32[24,16,128]{2,0,1:T(8,128)} %get-tuple-element.62) | copy-start | bytes 589828
  89.3 2.6 %copy-start.9 = (f32[24,16,128]{2,0,1:T(8,128)S(1)}, f32[24,16,128]{2,0,1:T(8,128)}, u32[]{:S(2)}) copy-start(f32[24,16,128]{2,0,1:T(8,128)} %get-tuple-element.63) | copy-start | bytes 589828
  89.3 2.6 %copy-start.10 = (f32[24,16,128]{2,0,1:T(8,128)S(1)}, f32[24,16,128]{2,0,1:T(8,128)}, u32[]{:S(2)}) copy-start(f32[24,16,128]{2,0,1:T(8,128)} %get-tuple-element.64) | copy-start | bytes 589828
  91.8 19.6 %copy-start.11 = (f32[2,24,16,128]{3,1,2,0:T(8,128)S(1)}, f32[2,24,16,128]{3,1,2,0:T(8,128)}, u32[]{:S(2)}) copy-start(f32[2,24,16,128]{3,1,2,0:T(8,128)} %fusion.105) | copy-start | bytes 1179652
  (36 other events, 69.1 us)
where the time goes:
time: 113 us
  other arithmetic  66.2 us (59%)
  starting transfers between devices  23.2 us (21%)
  waiting for transfers between devices  13.1 us (12%)
  local copies, waits for them, and re-layouts  9.19 us (8%)
    add x4, other arithmetic, shifted_sum(): total = outer if total is None else total + outer  46.1 us
    ppermute x4, starting transfers between devices, padded_2(): lax.ppermute(head, axis, [((i + 1) % count, i) for i in range(count)])  17.2 us
    ppermute x4, waiting for transfers between devices, padded_2(): lax.ppermute(head, axis, [((i + 1) % count, i) for i in range(count)])  13.1 us
    mul x6, other arithmetic, shifted_sum(): term = col_weight * piece  8.56 us
    ppermute x4, starting transfers between devices, padded_2(): lax.ppermute(tail, axis, [(i, (i + 1) % count) for i in range(count)])  5.99 us
    mul x3, other arithmetic, shifted_sum(): outer = row_weight * inner  4.6 us
    select_n x2, other arithmetic, clear_bands(): return jnp.where(inside[:, None], padded, 0.0)  3.96 us
    unnamed x124, local copies, waits for them, and re-layouts  3.07 us
  transfers between devices with their start and end apart: 8, of which 1 were waited for; matrix products, arithmetic and copies ran while one was open for 43% of the time, Pallas kernels for 0%

commit v1 on v0

v1 whole, which is shorter than its diff:
```python
import functools

import jax
import jax.numpy as jnp
from jax import lax
from jax.experimental import pallas as pl
from jax.experimental.pallas import tpu as pltpu
from jax.sharding import PartitionSpec as P

LEVS = 24
ROWS = 16
COLS = 128
FIELDS = 6
GROUPS = 3
PAIRS = FIELDS * LEVS // 2
EDGE = FIELDS * GROUPS
T_EDGE = 8 * (PAIRS + 2)
T_ROWS = T_EDGE + 8 * (2 * EDGE // 4)
PAD_ROWS = 32
VMEM_LIMIT = 48 * 1024 * 1024


def parities():
    return lax.axis_index("lon") % 2 == 0, lax.axis_index("lat") % 2 == 0


def pick(flag, first, second):
    return jnp.where(jnp.full(first.shape, flag), first, second)


def lane_slot(shape):
    return lax.broadcasted_iota(jnp.int32, shape, len(shape) - 1) % 16


def pack_kernel(wind_ref, tracer_ref, sa_ref, sb_ref, t1_ref, t2_ref):
    lon_even, lat_even = parities()
    low_half = lax.broadcasted_iota(jnp.int32, (8, COLS), 0) < 4
    zero = jnp.zeros((8, COLS), jnp.float32)
    for t_ref in (t1_ref, t2_ref):
        t_ref[0:8] = zero
        t_ref[8 * (PAIRS + 1) : T_EDGE] = zero

    def field_rows(ref, base, count):
        def step(pair, carry):
            field = pair // (LEVS // 2)
            lev = 2 * (pair % (LEVS // 2))
            first = ref[field, lev]
            second = ref[field, lev + 1]
            top = jnp.where(low_half, first[0:8], pltpu.roll(second[0:8], 4, 0))
            bottom = jnp.where(low_half, pltpu.roll(first[8:16], 4, 0), second[8:16])
            start = pl.multiple_of(8 * (base + pair + 1), 8)
            t1_ref[pl.ds(start, 8)] = pick(lat_even, bottom, top)
            t2_ref[pl.ds(start, 8)] = pick(lat_even, top, bottom)
            return carry

        lax.fori_loop(0, count, step, 0, unroll=4)

    field_rows(wind_ref, 0, LEVS)
    field_rows(tracer_ref, LEVS, 2 * LEVS)
    for field in range(FIELDS):
        ref, inner = (wind_ref, field) if field < 2 else (tracer_ref, field - 2)
        for group in range(GROUPS):
            turned = ref[inner, 8 * group : 8 * group + 8].reshape(COLS, COLS).T
            west = turned[0:8]
            east = turned[COLS - 8 : COLS]
            sa_ref[GROUPS * field + group] = pick(lon_even, east, west)
            sb_ref[GROUPS * field + group] = pick(lon_even, west, east)


def corner_kernel(sa_ref, sb_ref, t1_in, t2_in, t1_ref, t2_ref, buf1, buf2, sem1, sem2):
    lon_even, lat_even = parities()
    slot = lane_slot((8, COLS))
    halos = []
    for edge in range(EDGE):
        halos.append(pick(lon_even, sb_ref[edge], sa_ref[edge]))
    for edge in range(EDGE):
        halos.append(pick(lon_even, sa_ref[edge], sb_ref[edge]))
    for packed in range(2 * EDGE // 4):
        top = None
        bottom = None
        for part in range(4):
            piece = halos[4 * packed + part]
            upper = pltpu.roll(piece, 4 * part, 1) if part else piece
            lower = pltpu.roll(piece, (4 * part - 12) % COLS, 1) if part != 3 else piece
            here = (slot >= 4 * part) & (slot < 4 * part + 4)
            top = upper if top is None else jnp.where(here, upper, top)
            bottom = lower if bottom is None else jnp.where(here, lower, bottom)
        buf1[8 * packed : 8 * packed + 8] = pick(lat_even, bottom, top)
        buf2[8 * packed : 8 * packed + 8] = pick(lat_even, top, bottom)
    copy1 = pltpu.make_async_copy(buf1, t1_ref.at[pl.ds(T_EDGE, T_ROWS - T_EDGE)], sem1)
    copy2 = pltpu.make_async_copy(buf2, t2_ref.at[pl.ds(T_EDGE, T_ROWS - T_EDGE)], sem2)
    copy1.start()
    copy2.start()
    copy1.wait()
    copy2.wait()


def cubic_weights(frac):
    return (
        -frac * (frac - 1.0) * (frac - 2.0) * (1.0 / 6.0),
        (frac + 1.0) * (frac - 1.0) * (frac - 2.0) * 0.5,
        (frac + 1.0) * frac * (frac - 2.0) * -0.5,
        (frac + 1.0) * frac * (frac - 1.0) * (1.0 / 6.0),
    )


def rotated(weights, odd, half):
    once = [jnp.where(odd, weights[(k - 1) % 4], weights[k]) for k in range(4)]
    return [jnp.where(half, once[(k - 2) % 4], once[k]) for k in range(4)]


def middle_pair(values, odd, half):
    one = jnp.where(half, values[3], values[1])
    two = jnp.where(half, values[0], values[2])
    three = jnp.where(half, values[1], values[3])
    return jnp.where(odd, two, one), jnp.where(odd, three, two)


def advect_block(load, col_off, row_off, wind_here, emit):
    row_start = 2 - row_off
    col_start = 6 - col_off
    row_low = [row_start <= p for p in range(4)]
    col_low = [col_start <= q for q in range(4)]
    col_mid = [col_start <= q + 4 for q in range(4)]
    row_odd = (row_start & 1) != 0
    row_half = (row_start & 2) != 0
    col_odd = (col_start & 1) != 0
    col_half = (col_start & 2) != 0

    def column_class(field, q):
        picked = []
        for p in range(4):
            parts = [
                jnp.where(row_low[p], load(field, p, k), load(field, p + 4, k))
                for k in (q, q + 4, q + 8)
            ]
            picked.append(
                jnp.where(col_low[q], parts[0], jnp.where(col_mid[q], parts[1], parts[2]))
            )
        return picked

    col_float = col_off.astype(jnp.float32)
    row_float = row_off.astype(jnp.float32)
    wind_taps = [[column_class(field, q) for q in range(4)] for field in range(2)]
    cells = []
    for field in range(2):
        lows = []
        highs = []
        for q in range(4):
            low, high = middle_pair(wind_taps[field][q], row_odd, row_half)
            lows.append(low)
            highs.append(high)
        low_left, low_right = middle_pair(lows, col_odd, col_half)
        up_left, up_right = middle_pair(highs, col_odd, col_half)
        cells.append((low_left, low_right - low_left, up_left, up_right - up_left))
    disp = wind_here
    for repeat in range(2):
        frac_x = jnp.clip(col_float - disp[0], 0.0, 1.0)
        frac_y = jnp.clip(row_float - disp[1], 0.0, 1.0)
        moved = []
        for field in range(2):
            low_left, low_step, up_left, up_step = cells[field]
            low = low_left + frac_x * low_step
            up = up_left + frac_x * up_step
            depart = low + frac_y * (up - low)
            moved.append(0.5 * (wind_here[field] + depart))
        disp = moved
    frac_x = jnp.clip(col_float - disp[0], 0.0, 1.0)
    frac_y = jnp.clip(row_float - disp[1], 0.0, 1.0)
    col_weights = rotated(cubic_weights(frac_x), col_odd, col_half)
    row_weights = rotated(cubic_weights(frac_y), row_odd, row_half)
    for field in range(FIELDS):
        sums = [None] * 4
        for q in range(4):
            taps = wind_taps[field][q] if field < 2 else column_class(field, q)
            for p in range(4):
                term = col_weights[q] * taps[p]
                sums[p] = term if sums[p] is None else sums[p] + term
        total = row_weights[0] * sums[0]
        for p in range(1, 4):
            total = total + row_weights[p] * sums[p]
        emit(field, total)


def main_kernel(
    wind_ref, tracer_ref, off_ref, sa_ref, sb_ref, t1_ref, t2_ref, out_ref, rows, halo, shifted, turned_off, turned_out
):
    lon_even, lat_even = parities()
    slot = lane_slot((8, COLS))

    def fill(ref, base, count):
        def step(index, carry):
            lev = index % LEVS
            whole = base + index
            own = ref[index // LEVS, lev]
            start = pl.multiple_of(whole * PAD_ROWS, PAD_ROWS)
            rows[pl.ds(start + 8, 16)] = own
            first = t1_ref[pl.ds(4 * whole + 4, 8)]
            second = t2_ref[pl.ds(4 * whole + 4, 8)]
            rows[pl.ds(start, 8)] = pick(lat_even, second, first)
            first = t1_ref[pl.ds(4 * whole + 8, 8)]
            second = t2_ref[pl.ds(4 * whole + 8, 8)]
            rows[pl.ds(start + 24, 8)] = pick(lat_even, first, second)
            return carry

        lax.fori_loop(0, count, step, 0, unroll=4)

    fill(wind_ref, 0, 2 * LEVS)
    fill(tracer_ref, 2 * LEVS, 4 * LEVS)
    for packed in range(2 * EDGE // 4):
        start = T_EDGE + 8 * packed
        first = t1_ref[start : start + 8]
        second = t2_ref[start : start + 8]
        north = pick(lat_even, second, first)
        south = pick(lat_even, first, second)
        for part in range(4):
            above = pltpu.roll(north, (-4 - 4 * part) % COLS, 1)
            below = pltpu.roll(south, 16 - 4 * part, 1)
            halo[4 * packed + part] = jnp.where(slot >= 12, above, below)

    def build(group, place, unit):
        field = unit // 8
        row = unit % 8
        base = (field * LEVS + 8 * group) * PAD_ROWS + row + 5
        block = jnp.concatenate([rows[pl.ds(base + lev * PAD_ROWS, 16)] for lev in range(8)], axis=0)
        shifted[place, field, row, 8 : 8 + COLS] = block.T
        edge = GROUPS * field + group
        outside = (slot < row - 3) | (slot > row + 12)
        from_a = sa_ref[edge]
        from_b = sb_ref[edge]
        west = jnp.where(outside, halo[edge], pick(lon_even, from_b, from_a))
        east = jnp.where(outside, halo[EDGE + edge], pick(lon_even, from_a, from_b))
        turn = (3 - row) % COLS
        shifted[place, field, row, 0:8] = pltpu.roll(west, turn, 1)
        shifted[place, field, row, 8 + COLS : 16 + COLS] = pltpu.roll(east, turn, 1)

    def build_off(group, place):
        for part in range(2):
            block = off_ref[part, 8 * group : 8 * group + 8].reshape(COLS, COLS)
            turned_off[place, part] = block.T

    def compute(place, block):
        start = pl.multiple_of(8 * block, 8)

        def load(field, row, k):
            return shifted[place, field, row, pl.ds(start + 1 + k, 8)]

        def emit(field, value):
            turned_out[field, pl.ds(start, 8)] = value

        here = [shifted[place, field, 3, pl.ds(start + 8, 8)] for field in range(2)]
        advect_block(
            load, turned_off[place, 0, pl.ds(start, 8)], turned_off[place, 1, pl.ds(start, 8)], here, emit
        )

    build_off(0, 0)

    def first_units(unit, carry):
        build(0, 0, unit)
        return carry

    lax.fori_loop(0, 48, first_units, 0, unroll=2)
    for group in range(GROUPS):
        place = group % 2
        last = group + 1 == GROUPS
        if not last:
            build_off(group + 1, 1 - place)

        def step(block, carry):
            if not last:
                for part in range(3):
                    build(group + 1, 1 - place, 3 * block + part)
            compute(place, block)
            return carry

        lax.fori_loop(0, 16, step, 0)
        for field in range(FIELDS):
            out_ref[field, 8 * group : 8 * group + 8] = turned_out[field].T.reshape(8, ROWS, COLS)


def shards(wind, tracers, cell_off):
    f32 = jnp.float32
    vmem = pl.BlockSpec(memory_space=pltpu.VMEM)
    anywhere = pl.BlockSpec(memory_space=pl.ANY)
    params = pltpu.CompilerParams(vmem_limit_bytes=VMEM_LIMIT)
    edge_shape = jax.ShapeDtypeStruct((EDGE, 8, COLS), f32)
    t_shape = jax.ShapeDtypeStruct((T_ROWS, COLS), f32)
    sa, sb, t1, t2 = pl.pallas_call(
        pack_kernel,
        out_shape=(edge_shape, edge_shape, t_shape, t_shape),
        in_specs=[vmem] * 2,
        out_specs=(vmem,) * 4,
        compiler_params=params,
        name="pack",
    )(wind, tracers)
    count = lax.axis_size("lon")
    lon_first = [(i, i ^ 1) for i in range(count)]
    lon_second = [(i, (i + 1) % count if i % 2 else (i - 1) % count) for i in range(count)]
    lats = lax.axis_size("lat")
    lat_first = [(i, i ^ 1) for i in range(lats)]
    lat_second = [(i, i + 1 if i % 2 else i - 1) for i in range(1, lats - 1)]
    sa = lax.ppermute(sa, "lon", lon_first)
    sb = lax.ppermute(sb, "lon", lon_second)
    t1, t2 = pl.pallas_call(
        corner_kernel,
        out_shape=(t_shape, t_shape),
        in_specs=[vmem, vmem, anywhere, anywhere],
        out_specs=(anywhere, anywhere),
        scratch_shapes=[
            pltpu.VMEM((T_ROWS - T_EDGE, COLS), f32),
            pltpu.VMEM((T_ROWS - T_EDGE, COLS), f32),
            pltpu.SemaphoreType.DMA,
            pltpu.SemaphoreType.DMA,
        ],
        input_output_aliases={2: 0, 3: 1},
        compiler_params=params,
        name="corners",
    )(sa, sb, t1, t2)
    t1 = lax.ppermute(t1, "lat", lat_first)
    t2 = lax.ppermute(t2, "lat", lat_second)
    return pl.pallas_call(
        main_kernel,
        out_shape=jax.ShapeDtypeStruct((FIELDS, LEVS, ROWS, COLS), f32),
        in_specs=[vmem] * 7,
        out_specs=vmem,
        scratch_shapes=[
            pltpu.VMEM((FIELDS * LEVS * PAD_ROWS, COLS), f32),
            pltpu.VMEM((2 * EDGE, 8, COLS), f32),
            pltpu.VMEM((2, FIELDS, 8, COLS + 16, COLS), f32),
            pltpu.VMEM((2, 2, COLS, COLS), jnp.int32),
            pltpu.VMEM((FIELDS, COLS, COLS), f32),
        ],
        compiler_params=params,
        name="advect",
    )(wind, tracers, cell_off, sa, sb, t1, t2)


def solution(mesh):
    placed = P(None, None, "lat", "lon")
    return jax.shard_map(shards, mesh=mesh, in_specs=(placed,) * 3, out_specs=placed, check_vma=False)
```

time: 113 us -> 45 us (0.40)
  other arithmetic: 66.2 us -> 0 us
  Pallas kernels: 0 us -> 19.1 us
  local copies, waits for them, and re-layouts: 9.19 us -> 2.14 us
  starting transfers between devices: 23.2 us -> 16.5 us
  waiting for transfers between devices: 13.1 us -> 7.02 us
    add x4 -> x0, other arithmetic: 46.1 us -> none  [shifted_sum(): total = outer if total is None else total + outer]
    pallas_call x0 -> x3, Pallas kernels: none -> 19.1 us  [the longest x1 17.9 us: shards(): pl.pallas_call(main_kernel, out_shape=jax.ShapeDtypeStruct((FIELDS, LEVS,...]
    mul x9 -> x0, other arithmetic: 13.2 us -> none  [the longest x6 8.56 us: shifted_sum(): term = col_weight * piece]
    ppermute x8 -> x4, starting transfers between devices: 23.2 us -> 16.5 us  [the longest x1 7.66 us: shards(): sb = lax.ppermute(sb, 'lon', lon_second)]
    ppermute x8 -> x4, waiting for transfers between devices: 13.1 us -> 7.02 us  [the longest x1 5.28 us: shards(): t2 = lax.ppermute(t2, 'lat', lat_second)]
    select_n x2 -> x0, other arithmetic: 3.96 us -> none  [clear_bands(): return jnp.where(inside[:, None], padded, 0.0)]
    ppermute x2 -> x0, local copies, waits for them, and re-layouts: 3.06 us -> none  [the longest x1 1.67 us: padded_2(): lax.ppermute(tail, axis, [(i, (i + 1) % count) for i in range(count)])]
    slice x2 -> x0, other arithmetic: 2.89 us -> none  [padded_2(): lax.slice_in_dim(cells, cells.shape[dim] - width, cells.shape[dim], axis=...]
  transfers between devices with their start and end apart: 8 -> 4, of which waited for: 1 -> 2; matrix products, arithmetic and copies ran while one was open for 43% -> 0% of each run, Pallas kernels for 0% -> 0%
where the time goes in v1:
time: 45 us; the launch traced here: 44.8 us
  Pallas kernels  19.1 us (42%)
  starting transfers between devices  16.5 us (37%)
  waiting for transfers between devices  7.02 us (16%)
  local copies, waits for them, and re-layouts  2.14 us (5%)
    pallas_call x1, Pallas kernels, shards(): pl.pallas_call(main_kernel, out_shape=jax.ShapeDtypeStruct((FIELDS, LEVS,...  17.9 us
    ppermute x1, starting transfers between devices, shards(): sb = lax.ppermute(sb, 'lon', lon_second)  7.66 us
    ppermute x1, waiting for transfers between devices, shards(): t2 = lax.ppermute(t2, 'lat', lat_second)  5.28 us
    ppermute x1, starting transfers between devices, shards(): t2 = lax.ppermute(t2, 'lat', lat_second)  4.72 us
    ppermute x1, starting transfers between devices, shards(): sa = lax.ppermute(sa, 'lon', lon_first)  2.21 us
    unnamed x10, local copies, waits for them, and re-layouts  2.14 us
    ppermute x1, starting transfers between devices, shards(): t1 = lax.ppermute(t1, 'lat', lat_first)  1.91 us
    ppermute x1, waiting for transfers between devices, shards(): sb = lax.ppermute(sb, 'lon', lon_second)  1.74 us
  transfers between devices with their start and end apart: 4, of which 2 were waited for; matrix products, arithmetic and copies ran while one was open for 0% of the time, Pallas kernels for 0%

profile of v1, /device:TPU:1, one launch (start us, length us, event | category | flops | bytes accessed | tf_op | source)
XLA Modules:
  0.0 44.8 jit_solution(1112265635607275610)
XLA Ops:
  0.0 0.0 copy-start
  0.0 1.1 %copy-done = f32[4,24,16,128]{3,2,1,0:T(8,128)S(1)} copy-done((f32[4,24,16,128]{3,2,1,0:T(8,128)S(1)}, f32[4,24,16,128]{3,2,1,0:T(8,128)}, u32[]{:S(2)}) %copy-start) | copy-done | bytes 786456
  1.1 0.0 copy-start.2
  1.1 1.0 %copy-done.2 = f32[2,24,16,128]{3,2,1,0:T(8,128)S(1)} copy-done((f32[2,24,16,128]{3,2,1,0:T(8,128)S(1)}, f32[2,24,16,128]{3,2,1,0:T(8,128)}, u32[]{:S(2)}) %copy-start.2) | copy-done | bytes 393240
  2.1 0.0 copy-start.1
  2.1 0.0 copy-start.3
  2.1 0.0 copy-start.4
  2.1 1.0 %pack.1 = (f32[18,8,128]{2,1,0:T(8,128)S(1)}, f32[18,8,128]{2,1,0:T(8,128)S(1)}, f32[664,128]{1,0:T(8,128)S(1)}, f32[664,128]{1,0:T(8,128)S(1)}) custom-call(f32[2,24,16,128]{3,2,1,0:T(8,128)S(1)} %copy-done.2, f32[4,24,16,128]{3,2,1,0:T(8,128)S(1)} %copy-done), custom_call_target="tpu_custom_call" | custom-call | tf_op jit(solution)/shard_map/pack/pallas_call | solution.py:288
  3.1 2.2 %collective-permute-start = (f32[18,8,128]{2,1,0:T(8,128)S(1)}, f32[18,8,128]{2,1,0:T(8,128)S(1)}, u32[]{:S(2)}, u32[]{:S(2)}) collective-permute-start(f32[18,8,128]{2,1,0:T(8,128)S(1)} %get-tuple-element.11), channel_id=1, source_target_pairs={{0,4},{4,0},{8,12},{12,8},{16,20},{20,16},{24,28},{28,24},{32,36},... | collective-permute-start | bytes 221192 | tf_op jit(solution)/shard_map/ppermute | solution.py:302
  5.3 7.7 %collective-permute-start.1 = (f32[18,8,128]{2,1,0:T(8,128)S(1)}, f32[18,8,128]{2,1,0:T(8,128)S(1)}, u32[]{:S(2)}, u32[]{:S(2)}) collective-permute-start(f32[18,8,128]{2,1,0:T(8,128)S(1)} %get-tuple-element.12), channel_id=1, source_target_pairs={{0,252},{4,8},{8,4},{12,16},{16,12},{20,24},{24,20},{28,32},{32,28... | collective-permute-start | bytes 221192 | tf_op jit(solution)/shard_map/ppermute | solution.py:303
  13.0 0.0 collective-permute-done.sa_ref
  13.0 1.7 %collective-permute-done.1.sb_ref = f32[18,8,128]{2,1,0:T(8,128)S(1)} collective-permute-done((f32[18,8,128]{2,1,0:T(8,128)S(1)}, f32[18,8,128]{2,1,0:T(8,128)S(1)}, u32[]{:S(2)}, u32[]{:S(2)}) %collective-permute-start.1) | collective-permute-done | bytes 73760 | tf_op jit(solution)/shard_map/ppermute | solution.py:303
  14.7 0.2 corners.1
  15.0 1.9 %collective-permute-start.2 = (f32[664,128]{1,0:T(8,128)S(1)}, f32[664,128]{1,0:T(8,128)S(1)}, u32[]{:S(2)}, u32[]{:S(2)}) collective-permute-start(f32[664,128]{1,0:T(8,128)S(1)} %get-tuple-element.15), channel_id=1, source_target_pairs={{0,1},{1,0},{2,3},{3,2},{4,5},{5,4},{6,7},{7,6},{8,9},{9,8},{10,11... | collective-permute-start | bytes 1019912 | tf_op jit(solution)/shard_map/ppermute | solution.py:319
  16.9 4.7 %collective-permute-start.3 = (f32[664,128]{1,0:T(8,128)S(1)}, f32[664,128]{1,0:T(8,128)S(1)}, u32[]{:S(2)}, u32[]{:S(2)}) collective-permute-start(f32[664,128]{1,0:T(8,128)S(1)} %get-tuple-element.16), channel_id=1, source_target_pairs={{1,2},{2,1},{5,6},{6,5},{9,10},{10,9},{13,14},{14,13},{17,18},{18,... | collective-permute-start | bytes 1019912 | tf_op jit(solution)/shard_map/ppermute | solution.py:320
  21.6 0.0 collective-permute-done.2.t1_ref
  21.6 5.3 %collective-permute-done.3.t2_ref = f32[664,128]{1,0:T(8,128)S(1)} collective-permute-done((f32[664,128]{1,0:T(8,128)S(1)}, f32[664,128]{1,0:T(8,128)S(1)}, u32[]{:S(2)}, u32[]{:S(2)}) %collective-permute-start.3) | collective-permute-done | bytes 340000 | tf_op jit(solution)/shard_map/ppermute | solution.py:320
  26.9 0.0 copy-done.1
  26.9 0.0 copy-done.3
  26.9 0.0 copy-done.4
  26.9 17.9 %advect.1 = f32[6,24,16,128]{3,2,1,0:T(8,128)} custom-call(f32[2,24,16,128]{3,2,1,0:T(8,128)S(1)} %copy-done.3, f32[4,24,16,128]{3,2,1,0:T(8,128)S(1)} %copy-done.1, s32[2,24,16,128]{3,2,1,0:T(8,128)S(1)} %copy-done.4, f32[18,8,128]{2,1,0:T(8,128)S(1)} %collective-permute-done.sa_ref, f32[18,8,128]{2,1,0:T(8,128)S(1)} %collective-permute-done.1.sb_ref, ...), custom_call_target="tpu_custom_call" | custom-call | tf_op jit(solution)/shard_map/advect/pallas_call | solution.py:321
Async XLA Ops:
  0.0 1.1 %copy-start = (f32[4,24,16,128]{3,2,1,0:T(8,128)S(1)}, f32[4,24,16,128]{3,2,1,0:T(8,128)}, u32[]{:S(2)}) copy-start(f32[4,24,16,128]{3,2,1,0:T(8,128)} %tracer_ref.3) | copy-start | bytes 2359300
  1.1 1.0 %copy-start.2 = (f32[2,24,16,128]{3,2,1,0:T(8,128)S(1)}, f32[2,24,16,128]{3,2,1,0:T(8,128)}, u32[]{:S(2)}) copy-start(f32[2,24,16,128]{3,2,1,0:T(8,128)} %wind_ref.3) | copy-start | bytes 1179652
  2.1 24.8 %copy-start.1 = (f32[4,24,16,128]{3,2,1,0:T(8,128)S(1)}, f32[4,24,16,128]{3,2,1,0:T(8,128)}, u32[]{:S(2)}) copy-start(f32[4,24,16,128]{3,2,1,0:T(8,128)} %tracer_ref.3) | copy-start | bytes 2359300
  2.1 24.8 %copy-start.3 = (f32[2,24,16,128]{3,2,1,0:T(8,128)S(1)}, f32[2,24,16,128]{3,2,1,0:T(8,128)}, u32[]{:S(2)}) copy-start(f32[2,24,16,128]{3,2,1,0:T(8,128)} %wind_ref.3) | copy-start | bytes 1179652
  2.1 24.8 %copy-start.4 = (s32[2,24,16,128]{3,2,1,0:T(8,128)S(1)}, s32[2,24,16,128]{3,2,1,0:T(8,128)}, u32[]{:S(2)}) copy-start(s32[2,24,16,128]{3,2,1,0:T(8,128)} %off_ref.1) | copy-start | bytes 1179652
  3.1 9.9 %collective-permute-start = (f32[18,8,128]{2,1,0:T(8,128)S(1)}, f32[18,8,128]{2,1,0:T(8,128)S(1)}, u32[]{:S(2)}, u32[]{:S(2)}) collective-permute-start(f32[18,8,128]{2,1,0:T(8,128)S(1)} %get-tuple-element.11), channel_id=1, source_target_pairs={{0,4},{4,0},{8,12},{12,8},{16,20},{20,16},{24,28},{28,24},{32,36},... | collective-permute-start | bytes 221192 | tf_op jit(solution)/shard_map/ppermute | solution.py:302
  5.3 9.4 %collective-permute-start.1 = (f32[18,8,128]{2,1,0:T(8,128)S(1)}, f32[18,8,128]{2,1,0:T(8,128)S(1)}, u32[]{:S(2)}, u32[]{:S(2)}) collective-permute-start(f32[18,8,128]{2,1,0:T(8,128)S(1)} %get-tuple-element.12), channel_id=1, source_target_pairs={{0,252},{4,8},{8,4},{12,16},{16,12},{20,24},{24,20},{28,32},{32,28... | collective-permute-start | bytes 221192 | tf_op jit(solution)/shard_map/ppermute | solution.py:303
  15.0 6.6 %collective-permute-start.2 = (f32[664,128]{1,0:T(8,128)S(1)}, f32[664,128]{1,0:T(8,128)S(1)}, u32[]{:S(2)}, u32[]{:S(2)}) collective-permute-start(f32[664,128]{1,0:T(8,128)S(1)} %get-tuple-element.15), channel_id=1, source_target_pairs={{0,1},{1,0},{2,3},{3,2},{4,5},{5,4},{6,7},{7,6},{8,9},{9,8},{10,11... | collective-permute-start | bytes 1019912 | tf_op jit(solution)/shard_map/ppermute | solution.py:319
  16.9 10.0 %collective-permute-start.3 = (f32[664,128]{1,0:T(8,128)S(1)}, f32[664,128]{1,0:T(8,128)S(1)}, u32[]{:S(2)}, u32[]{:S(2)}) collective-permute-start(f32[664,128]{1,0:T(8,128)S(1)} %get-tuple-element.16), channel_id=1, source_target_pairs={{1,2},{2,1},{5,6},{6,5},{9,10},{10,9},{13,14},{14,13},{17,18},{18,... | collective-permute-start | bytes 1019912 | tf_op jit(solution)/shard_map/ppermute | solution.py:320

commit v2 on v1

v2 whole, which is shorter than its diff:
```python
import jax
import jax.numpy as jnp
from jax import lax
from jax.experimental import pallas as pl
from jax.experimental.pallas import tpu as pltpu
from jax.sharding import PartitionSpec as P

LEVS = 24
ROWS = 16
COLS = 128
WINDS = 2
FIELDS = 6
GROUPS = 3
EDGE = FIELDS * GROUPS
WIDE = COLS + 16
DEPTH = 3 * COLS
SIDE = -(-EDGE // 4)
MAIN = 8 * (FIELDS * LEVS // 2 + 2)
NARROW = 2 * 8 * SIDE
PAYLOAD = EDGE + 2 * SIDE
STRIP = 24
TALL = COLS + 8
EARLY = 16
VMEM_LIMIT = 24 * 1024 * 1024
PACK_LIMIT = 60 * 1024 * 1024


def parities():
    return lax.axis_index("lon") % 2 == 0, lax.axis_index("lat") % 2 == 0


def pick(flag, first, second):
    return jnp.where(jnp.full(first.shape, flag), first, second)


def lane_slot(shape):
    return lax.broadcasted_iota(jnp.int32, shape, len(shape) - 1) % 16


def split(values):
    high = values.astype(jnp.bfloat16)
    return high, (values - high.astype(jnp.float32)).astype(jnp.bfloat16)


def whole(values):
    return values.astype(jnp.bfloat16).astype(jnp.float32)


def load_fields(wind_hbm, tracer_hbm, cells, sems):
    copies = []
    for field in range(FIELDS):
        source = wind_hbm.at[field] if field < WINDS else tracer_hbm.at[field - WINDS]
        copies.append(pltpu.make_async_copy(source, cells.at[field], sems.at[field]))
    for copy in copies:
        copy.start()
    return copies


def pack_kernel(wind_hbm, tracer_hbm, edges, t1_ref, t2_ref, cells, sems):
    lat_even = parities()[1]
    low_half = lax.broadcasted_iota(jnp.int32, (8, COLS), 0) < 4
    slot = lane_slot((8, COLS))
    zero = jnp.zeros((8, COLS), jnp.float32)
    copies = load_fields(wind_hbm, tracer_hbm, cells, sems)

    def put(start, top, bottom):
        t1_ref[start : start + 8] = pick(lat_even, bottom, top)
        t2_ref[start : start + 8] = pick(lat_even, top, bottom)

    put(0, zero, zero)
    put(MAIN - 8, zero, zero)
    for field in range(FIELDS):
        copies[field].wait()
        for group in range(GROUPS):
            turned = cells[field, 8 * group : 8 * group + 8].reshape(COLS, COLS).T
            edges[GROUPS * field + group] = turned[0:8]
            edges[EDGE + GROUPS * field + group] = turned[COLS - 8 : COLS]
        for pair in range(LEVS // 2):
            first = cells[field, 2 * pair]
            second = cells[field, 2 * pair + 1]
            top = jnp.where(low_half, first[0:8], pltpu.roll(second[0:8], 4, 0))
            bottom = jnp.where(low_half, pltpu.roll(first[8:16], 4, 0), second[8:16])
            put(8 * (field * LEVS // 2 + pair + 1), top, bottom)
    for side in range(2):
        for packed in range(SIDE):
            top = None
            bottom = None
            for part in range(min(4, EDGE - 4 * packed)):
                piece = edges[EDGE * side + 4 * packed + part]
                upper = pltpu.roll(piece, 4 * part, 1) if part else piece
                lower = pltpu.roll(piece, (4 * part - 12) % COLS, 1) if part != 3 else piece
                here = (slot >= 4 * part) & (slot < 4 * part + 4)
                top = upper if top is None else jnp.where(here, upper, top)
                bottom = lower if bottom is None else jnp.where(here, lower, bottom)
            put(MAIN + 8 * (SIDE * side + packed), top, bottom)


def side_kernel(edges, t1_ref, t2_ref, a_ref, forth_ref, back_ref):
    lon_even, lat_even = parities()

    def put(place, west, east):
        a_ref[place] = pick(lon_even, east, west)
        other = pick(lon_even, west, east)
        forth_ref[place] = other
        back_ref[place] = other

    for edge in range(EDGE):
        put(edge, edges[edge], edges[EDGE + edge])
    for packed in range(SIDE):
        north = []
        south = []
        for side in range(2):
            start = MAIN + 8 * (SIDE * side + packed)
            first = t1_ref[start : start + 8]
            second = t2_ref[start : start + 8]
            north.append(pick(lat_even, second, first))
            south.append(pick(lat_even, first, second))
        put(EDGE + packed, *north)
        put(EDGE + SIDE + packed, *south)


def own_kernel(wind_ref, tracer_ref, off_ref, own_ref, turned_off, matrix_ref):
    for field in range(FIELDS):
        ref, inner = (wind_ref, field) if field < WINDS else (tracer_ref, field - WINDS)
        for group in range(GROUPS):
            turned = ref[inner, 8 * group : 8 * group + 8].reshape(COLS, COLS).T
            own_ref[GROUPS * field + group] = jnp.concatenate(split(turned), axis=1)
    source = lax.broadcasted_iota(jnp.int32, (COLS, COLS), 0)
    target = lax.broadcasted_iota(jnp.int32, (COLS, COLS), 1)
    source_slot = source % 16
    beside = jnp.where(source_slot < 8, 16 + source_slot % 4, source_slot % 4 - 4)
    same = source // 16 == target // 16
    for shift in range(8):
        wanted = target % 16 + (shift - 3)
        inside = jnp.where(same & (source_slot == wanted), 1.0, 0.0).astype(jnp.bfloat16)
        outside = jnp.where(same & (beside == wanted), 1.0, 0.0).astype(jnp.bfloat16)
        lanes = slice(shift * COLS, (shift + 1) * COLS)
        matrix_ref[0:COLS, lanes] = inside
        matrix_ref[COLS : 2 * COLS, lanes] = inside
        matrix_ref[2 * COLS : DEPTH, lanes] = outside
    for part in range(2):
        for group in range(GROUPS):
            start = (GROUPS * part + group) * COLS
            turned_off[start : start + COLS] = off_ref[part, 8 * group : 8 * group + 8].reshape(COLS, COLS).T


def cubic_weights(frac):
    return (
        -frac * (frac - 1.0) * (frac - 2.0) * (1.0 / 6.0),
        (frac + 1.0) * (frac - 1.0) * (frac - 2.0) * 0.5,
        (frac + 1.0) * frac * (frac - 2.0) * -0.5,
        (frac + 1.0) * frac * (frac - 1.0) * (1.0 / 6.0),
    )


def rotated(weights, odd, half):
    once = [jnp.where(odd, weights[(k - 1) % 4], weights[k]) for k in range(4)]
    return [jnp.where(half, once[(k - 2) % 4], once[k]) for k in range(4)]


def middle_pair(values, odd, half):
    one = jnp.where(half, values[3], values[1])
    two = jnp.where(half, values[0], values[2])
    three = jnp.where(half, values[1], values[3])
    return jnp.where(odd, two, one), jnp.where(odd, three, two)


def weighted(taps, col_weights, row_weights):
    sums = [None] * 4
    for q in range(4):
        for p in range(4):
            term = col_weights[q] * taps[q][p]
            sums[p] = term if sums[p] is None else sums[p] + term
    total = row_weights[0] * sums[0]
    for p in range(1, 4):
        total = total + row_weights[p] * sums[p]
    return total


def advect_block(load, col_off, row_off, wind_here, emit):
    row_start = 2 - row_off
    col_start = 6 - col_off
    row_low = [row_start <= p for p in range(4)]
    col_low = [col_start <= q for q in range(4)]
    col_mid = [col_start <= q + 4 for q in range(4)]
    row_odd = (row_start & 1) != 0
    row_half = (row_start & 2) != 0
    col_odd = (col_start & 1) != 0
    col_half = (col_start & 2) != 0
    col_float = col_off.astype(jnp.float32)
    row_float = row_off.astype(jnp.float32)

    def column_class(field, q):
        picked = []
        for p in range(4):
            parts = [
                jnp.where(row_low[p], load(field, p, k), load(field, p + 4, k))
                for k in (q, q + 4, q + 8)
            ]
            picked.append(
                jnp.where(col_low[q], parts[0], jnp.where(col_mid[q], parts[1], parts[2]))
            )
        return picked

    wind_taps = [[column_class(field, q) for q in range(4)] for field in range(WINDS)]
    cells = []
    for field in range(WINDS):
        lows = []
        highs = []
        for q in range(4):
            low, high = middle_pair(wind_taps[field][q], row_odd, row_half)
            lows.append(low)
            highs.append(high)
        low_left, low_right = middle_pair(lows, col_odd, col_half)
        up_left, up_right = middle_pair(highs, col_odd, col_half)
        cells.append((low_left, low_right - low_left, up_left, up_right - up_left))
    disp = wind_here
    for repeat in range(2):
        frac_x = jnp.clip(col_float - disp[0], 0.0, 1.0)
        frac_y = jnp.clip(row_float - disp[1], 0.0, 1.0)
        moved = []
        for field in range(WINDS):
            low_left, low_step, up_left, up_step = cells[field]
            low = low_left + frac_x * low_step
            up = up_left + frac_x * up_step
            depart = low + frac_y * (up - low)
            moved.append(0.5 * (wind_here[field] + depart))
        disp = moved
    frac_x = jnp.clip(col_float - disp[0], 0.0, 1.0)
    frac_y = jnp.clip(row_float - disp[1], 0.0, 1.0)
    col_weights = rotated(cubic_weights(frac_x), col_odd, col_half)
    row_weights = rotated(cubic_weights(frac_y), row_odd, row_half)
    for field in range(FIELDS):
        if field < WINDS:
            taps = wind_taps[field]
        else:
            taps = [column_class(field, q) for q in range(4)]
        emit(field, weighted(taps, col_weights, row_weights))


def block_access(shifted, base, height):
    def load(field, row, k):
        return shifted[pl.ds(base + ((GROUPS * 8 * field + row) * height + 1 + k), 8)]

    here = [load(field, 3, 7) for field in range(WINDS)]
    return load, here


def interior(own_ref, off_ref, matrix_ref, t1_ref, t2_ref, result, beside, around, shifted):
    lat_even = parities()[1]
    low_half = lax.broadcasted_iota(jnp.int32, (8, COLS), 0) < 4
    for edge in range(EDGE):
        field, group = divmod(edge, GROUPS)
        pieces = []
        for lev in range(8):
            line = 4 * (field * LEVS + 8 * group + lev)
            one = [t_ref[line + 8 : line + 16] for t_ref in (t1_ref, t2_ref)]
            two = [t_ref[line + 4 : line + 12] for t_ref in (t1_ref, t2_ref)]
            south_one = pick(lat_even, one[0], one[1])
            south_two = pick(lat_even, two[0], two[1])
            north_one = pick(lat_even, one[1], one[0])
            north_two = pick(lat_even, two[1], two[0])
            pieces.append(jnp.where(low_half, whole(south_one), south_two - whole(south_two)))
            pieces.append(jnp.where(low_half, north_one - whole(north_one), whole(north_two)))
        turned = jnp.concatenate(pieces, axis=0).T.astype(jnp.bfloat16)
        around[edge] = turned
        beside[edge, 0:16] = turned[0:16]
        beside[edge, 16:32] = turned[COLS - 16 : COLS]
    for pair in range(4):
        lanes = slice(2 * COLS * pair, 2 * COLS * (pair + 1))
        rows = jnp.concatenate([own_ref[...], around[...]], axis=2).reshape(EDGE * COLS, DEPTH)
        spread = jnp.dot(rows, matrix_ref[:, lanes], preferred_element_type=jnp.float32)
        for edge in range(EDGE):
            for half in range(2):
                start = (8 * edge + 2 * pair + half) * TALL
                shifted[start : start + COLS] = spread[
                    edge * COLS : (edge + 1) * COLS, half * COLS : (half + 1) * COLS
                ]

    def step(index, carry):
        group = index // 14
        start = 8 * (index % 14)
        load, here = block_access(shifted, group * (8 * TALL) + start, TALL)
        place = pl.multiple_of(group * COLS + start + 8, 8)

        def emit(field, value):
            result[pl.ds(pl.multiple_of(place + GROUPS * COLS * field, 8), 8)] = value

        advect_block(load, off_ref[pl.ds(place, 8)], off_ref[pl.ds(pl.multiple_of(place + GROUPS * COLS, 8), 8)], here, emit)
        return carry

    lax.fori_loop(0, GROUPS * 14, step, 0, unroll=3)


def early_kernel(own_ref, off_ref, matrix_ref, t1_ref, t2_ref, back_in, result, beside, back_out, around, shifted):
    @pl.when(lax.axis_index("lon") % EARLY == 0)
    def _():
        interior(own_ref, off_ref, matrix_ref, t1_ref, t2_ref, result, beside, around, shifted)


def late_kernel(
    own_ref, off_ref, matrix_ref, t1_ref, t2_ref, forth, result_in, beside_in, result, beside, around, shifted
):
    early = lax.axis_index("lon") % EARLY == 0

    @pl.when(early)
    def _():
        result[...] = result_in[...]
        beside[...] = beside_in[...]

    @pl.when(jnp.logical_not(early))
    def _():
        interior(own_ref, off_ref, matrix_ref, t1_ref, t2_ref, result, beside, around, shifted)


def edge_work(
    own_ref, off_ref, matrix_ref, beside, result, a_ref, forth_ref, back_ref, out_ref, rows, shifted, staged, sems
):
    lon_even = parities()[0]
    slot = lane_slot((8, COLS))

    def sides(place):
        west = forth_ref[place] if back_ref is None else pick(lon_even, forth_ref[place], a_ref[place])
        east = a_ref[place] if back_ref is None else pick(lon_even, a_ref[place], back_ref[place])
        return west, east

    for packed in range(SIDE):
        north = sides(EDGE + packed)
        south = sides(EDGE + SIDE + packed)
        for part in range(min(4, EDGE - 4 * packed)):
            edge = 4 * packed + part
            outer = []
            for side in range(2):
                above = pltpu.roll(north[side], 12 - 4 * part, 1) if part != 3 else north[side]
                below = pltpu.roll(south[side], -4 * part % COLS, 1) if part else south[side]
                both = jnp.where(slot >= 12, above, below)
                rest = both - whole(both)
                rest = jnp.where(slot < 8, pltpu.roll(rest, 4, 1), pltpu.roll(rest, COLS - 4, 1))
                outer.append(jnp.where((slot >= 4) & (slot < 12), rest, both))
            rows[edge, 0:16, 0 : 2 * COLS] = own_ref[edge, 0:16]
            rows[edge, 16:32, 0 : 2 * COLS] = own_ref[edge, COLS - 16 : COLS]
            rows[edge, 0:32, 2 * COLS : DEPTH] = beside[edge]
            rows[edge, 32:48, 0 : 2 * COLS] = jnp.concatenate(
                split(jnp.concatenate(sides(edge), axis=0)), axis=1
            )
            rows[edge, 32:48, 2 * COLS : DEPTH] = jnp.concatenate(outer, axis=0).astype(jnp.bfloat16)
    for pair in range(4):
        lanes = slice(2 * COLS * pair, 2 * COLS * (pair + 1))
        spread = jnp.dot(
            rows[...].reshape(EDGE * 2 * STRIP, DEPTH), matrix_ref[:, lanes], preferred_element_type=jnp.float32
        )
        for edge in range(EDGE):
            for half in range(2):
                part = spread[edge * 2 * STRIP : (edge + 1) * 2 * STRIP, half * COLS : (half + 1) * COLS]
                start = (8 * edge + 2 * pair + half) * 2 * STRIP
                shifted[start : start + 8] = part[32:40]
                shifted[start + 8 : start + 40] = part[0:32]
                shifted[start + 40 : start + 48] = part[40:48]

    copies = []
    for group in range(GROUPS):
        values = {}
        for side in range(2):
            target = (COLS - 8) * side + COLS * group
            other = target + GROUPS * COLS
            load, here = block_access(shifted, (16 * group + side) * STRIP, 2 * STRIP)

            def emit(field, value):
                values[field, side] = value

            advect_block(load, off_ref[target : target + 8], off_ref[other : other + 8], here, emit)
        for field in range(FIELDS):
            start = (GROUPS * field + group) * COLS
            whole_block = jnp.concatenate(
                [values[field, 0], result[start + 8 : start + COLS - 8], values[field, 1]], axis=0
            )
            staged[group, field] = whole_block.T.reshape(8, ROWS, COLS)
            copies.append(
                pltpu.make_async_copy(
                    staged.at[group, field], out_ref.at[field, pl.ds(8 * group, 8)], sems.at[group, field]
                )
            )
            copies[-1].start()
    for copy in copies:
        copy.wait()


def early_edge_kernel(own_ref, off_ref, matrix_ref, beside, result, a_ref, forth_ref, out_ref, *scratch):
    @pl.when(lax.axis_index("lon") % EARLY == 0)
    def _():
        edge_work(own_ref, off_ref, matrix_ref, beside, result, a_ref, forth_ref, None, out_ref, *scratch)


def late_edge_kernel(
    own_ref, off_ref, matrix_ref, beside, result, a_ref, forth_ref, back_ref, out_in, out_ref, *scratch
):
    @pl.when(lax.axis_index("lon") % EARLY != 0)
    def _():
        edge_work(own_ref, off_ref, matrix_ref, beside, result, a_ref, forth_ref, back_ref, out_ref, *scratch)


def cost(flops):
    return pl.CostEstimate(flops=flops, bytes_accessed=10**6, transcendentals=0)


def shards(wind, tracers, cell_off):
    f32 = jnp.float32
    vmem = pl.BlockSpec(memory_space=pltpu.VMEM)
    anywhere = pl.BlockSpec(memory_space=pl.ANY)
    params = pltpu.CompilerParams(vmem_limit_bytes=VMEM_LIMIT)
    sds = jax.ShapeDtypeStruct
    hbm = pl.BlockSpec(memory_space=pltpu.HBM)
    hbm = pl.BlockSpec(memory_space=pltpu.HBM)
    direct = pltpu.CompilerParams(vmem_limit_bytes=PACK_LIMIT)
    lat_shape = sds((MAIN + NARROW, COLS), f32)
    cells_shape = pltpu.VMEM((FIELDS, LEVS, ROWS, COLS), f32)
    edges, t1, t2 = pl.pallas_call(
        pack_kernel,
        out_shape=(sds((2 * EDGE, 8, COLS), f32), lat_shape, lat_shape),
        in_specs=[hbm] * 2,
        out_specs=(vmem,) * 3,
        scratch_shapes=[cells_shape, pltpu.SemaphoreType.DMA((FIELDS,))],
        compiler_params=direct,
        name="pack",
    )(wind, tracers)
    count = lax.axis_size("lon")
    lon_pairs = [(i, i ^ 1) for i in range(count)]
    lon_forth = [(i, (i + 1) % count) for i in range(1, count, 2)]
    lon_back = [(i, (i - 1) % count) for i in range(0, count, 2)]
    lats = lax.axis_size("lat")
    lat_pairs = [(i, i ^ 1) for i in range(lats)]
    lat_middle = [(i, i + 1 if i % 2 else i - 1) for i in range(1, lats - 1)]
    t1 = lax.ppermute(t1, "lat", lat_pairs)
    t2 = lax.ppermute(t2, "lat", lat_middle)
    own, turned_off, matrix = pl.pallas_call(
        own_kernel,
        out_shape=(
            sds((EDGE, COLS, 2 * COLS), jnp.bfloat16),
            sds((2 * GROUPS * COLS, COLS), jnp.int32),
            sds((DEPTH, 8 * COLS), jnp.bfloat16),
        ),
        in_specs=[vmem] * 3,
        out_specs=(vmem,) * 3,
        compiler_params=params,
        cost_estimate=cost(2 * 10**10),
        name="own",
    )(wind, tracers, cell_off)
    side_shape = sds((PAYLOAD, 8, COLS), f32)
    side_a, forth, back = pl.pallas_call(
        side_kernel,
        out_shape=(side_shape,) * 3,
        in_specs=[vmem] * 3,
        out_specs=(vmem,) * 3,
        compiler_params=params,
        name="sides",
    )(edges, t1, t2)
    side_a = lax.ppermute(side_a, "lon", lon_pairs)
    forth = lax.ppermute(forth, "lon", lon_forth)
    result_shapes = (sds((EDGE * COLS, COLS), f32), sds((EDGE, 32, COLS), jnp.bfloat16))
    scratch = [pltpu.VMEM((EDGE, COLS, COLS), jnp.bfloat16), pltpu.VMEM((EDGE * 8 * TALL, COLS), f32)]
    result, beside, back = pl.pallas_call(
        early_kernel,
        out_shape=result_shapes + (side_shape,),
        in_specs=[vmem] * 5 + [anywhere],
        out_specs=(vmem, vmem, anywhere),
        scratch_shapes=scratch,
        input_output_aliases={5: 2},
        compiler_params=params,
        cost_estimate=cost(10**10),
        name="early",
    )(own, turned_off, matrix, t1, t2, back)
    back = lax.ppermute(back, "lon", lon_back)
    edge_scratch = [
        pltpu.VMEM((EDGE, 2 * STRIP, DEPTH), jnp.bfloat16),
        pltpu.VMEM((EDGE * 8 * 2 * STRIP, COLS), f32),
        pltpu.VMEM((GROUPS, FIELDS, 8, ROWS, COLS), f32),
        pltpu.SemaphoreType.DMA((GROUPS, FIELDS)),
    ]
    out = pl.pallas_call(
        early_edge_kernel,
        out_shape=sds((FIELDS, LEVS, ROWS, COLS), f32),
        in_specs=[vmem] * 7,
        out_specs=anywhere,
        scratch_shapes=edge_scratch,
        compiler_params=params,
        cost_estimate=cost(10**10),
        name="early_edges",
    )(own, turned_off, matrix, beside, result, side_a, forth)
    result, beside = pl.pallas_call(
        late_kernel,
        out_shape=result_shapes,
        in_specs=[vmem] * 5 + [anywhere] + [vmem] * 2,
        out_specs=(vmem, vmem),
        scratch_shapes=scratch,
        compiler_params=params,
        cost_estimate=cost(10**10),
        name="late",
    )(own, turned_off, matrix, t1, t2, forth, result, beside)
    return pl.pallas_call(
        late_edge_kernel,
        out_shape=sds((FIELDS, LEVS, ROWS, COLS), f32),
        in_specs=[vmem] * 8 + [anywhere],
        out_specs=anywhere,
        scratch_shapes=edge_scratch,
        input_output_aliases={8: 0},
        compiler_params=params,
        name="late_edges",
    )(own, turned_off, matrix, beside, result, side_a, forth, back, out)


def solution(mesh):
    placed = P(None, None, "lat", "lon")
    return jax.shard_map(shards, mesh=mesh, in_specs=(placed,) * 3, out_specs=placed, check_vma=False)
```

time: 45 us -> 35.2 us (0.78)
  the two profiles are of different devices: /device:TPU:1 before, /device:TPU:144 now
where the time goes in v2:
time: 35.2 us; the launch traced here: 35 us
  Pallas kernels  15.1 us (43%)
  starting transfers between devices  10.6 us (30%)
  waiting for transfers between devices  8.12 us (23%)
  local copies, waits for them, and re-layouts  1 us (3%)
    pallas_call x1, Pallas kernels, shards(): pl.pallas_call(late_kernel, out_shape=result_shapes, in_specs=[vmem] * 5...  8.21 us
    ppermute x1, waiting for transfers between devices, shards(): t2 = lax.ppermute(t2, 'lat', lat_middle)  7.42 us
    ppermute x1, starting transfers between devices, shards(): back = lax.ppermute(back, 'lon', lon_back)  3.61 us
    pallas_call x1, Pallas kernels, shards(): pl.pallas_call(late_edge_kernel, out_shape=sds((FIELDS, LEVS, ROWS, COLS)...  3.19 us
    ppermute x1, starting transfers between devices, shards(): side_a = lax.ppermute(side_a, 'lon', lon_pairs)  3.19 us
    pallas_call x1, Pallas kernels, shards(): pl.pallas_call(pack_kernel, out_shape=(sds((2 * EDGE, 8, COLS), f32), lat...  2.8 us
    ppermute x1, starting transfers between devices, shards(): t2 = lax.ppermute(t2, 'lat', lat_middle)  2.46 us
    ppermute x1, starting transfers between devices, shards(): forth = lax.ppermute(forth, 'lon', lon_forth)  1.29 us
  transfers between devices with their start and end apart: 5, of which 2 were waited for; matrix products, arithmetic and copies ran while one was open for 0% of the time, Pallas kernels for 26%

profile of v2, /device:TPU:144, one launch (start us, length us, event | category | flops | bytes accessed | tf_op | source)
XLA Modules:
  0.0 35.0 jit_solution(11734468488762290908)
XLA Ops:
  0.0 0.0 copy-start.1
  0.0 0.0 copy-start
  0.0 2.8 %pack.1 = (f32[36,8,128]{2,1,0:T(8,128)}, f32[672,128]{1,0:T(8,128)}, f32[672,128]{1,0:T(8,128)}) custom-call(f32[2,24,16,128]{3,2,1,0:T(8,128)} %wind_hbm.1, f32[4,24,16,128]{3,2,1,0:T(8,128)} %tracer_hbm.1), custom_call_target="tpu_custom_call" | custom-call | tf_op jit(solution)/shard_map/pack/pallas_call | solution.py:417
  2.8 0.1 collective-permute-start
  2.9 0.0 copy-start.2
  2.9 2.5 %collective-permute-start.1 = (f32[672,128]{1,0:T(8,128)}, f32[672,128]{1,0:T(8,128)S(1)}, u32[]{:S(2)}, u32[]{:S(2)}) collective-permute-start(f32[672,128]{1,0:T(8,128)} %get-tuple-element.23), channel_id=1, source_target_pairs={{1,2},{2,1},{5,6},{6,5},{9,10},{10,9},{13,14},{14,13},{17,18},{18,... | collective-permute-start | bytes 1032200 | tf_op jit(solution)/shard_map/ppermute | solution.py:434
  5.4 0.0 copy-done.1
  5.4 0.0 copy-done
  5.4 0.0 copy-start.3
  5.4 1.0 %copy-done.3 = s32[2,24,16,128]{3,2,1,0:T(8,128)S(1)} copy-done((s32[2,24,16,128]{3,2,1,0:T(8,128)S(1)}, s32[2,24,16,128]{3,2,1,0:T(8,128)}, u32[]{:S(2)}) %copy-start.3) | copy-done | bytes 393240
  6.4 0.7 %own.1 = (bf16[18,128,256]{2,1,0:T(8,128)(2,1)S(1)}, s32[768,128]{1,0:T(8,128)S(1)}, bf16[384,1024]{1,0:T(8,128)(2,1)S(1)}) custom-call(f32[2,24,16,128]{3,2,1,0:T(8,128)S(1)} %copy-done.1, f32[4,24,16,128]{3,2,1,0:T(8,128)S(1)} %copy-done, s32[2,24,16,128]{3,2,1,0:T(8,128)S(1)} %copy-done.3), custom_call_target="tpu_custom_call" | custom-call | flops 20000000000 | bytes 1000000 | tf_op jit(solution)/shard_map/own/pallas_call | solution.py:435
  7.1 0.0 collective-permute-done.t1_ref
  7.1 7.4 %collective-permute-done.1.t2_ref = f32[672,128]{1,0:T(8,128)S(1)} collective-permute-done((f32[672,128]{1,0:T(8,128)}, f32[672,128]{1,0:T(8,128)S(1)}, u32[]{:S(2)}, u32[]{:S(2)}) %collective-permute-start.1) | collective-permute-done | bytes 344096 | tf_op jit(solution)/shard_map/ppermute | solution.py:434
  14.6 0.0 copy-done.2
  14.6 1.3 %collective-permute-start.2 = (f32[28,8,128]{2,1,0:T(8,128)S(1)}, f32[28,8,128]{2,1,0:T(8,128)S(1)}, u32[]{:S(2)}, u32[]{:S(2)}) collective-permute-start(f32[28,8,128]{2,1,0:T(8,128)S(1)} %get-tuple-element.25), channel_id=1, source_target_pairs={{4,8},{12,16},{20,24},{28,32},{36,40},{44,48},{52,56},{60,64},{68,... | collective-permute-start | bytes 344072 | tf_op jit(solution)/shard_map/ppermute | solution.py:458
  15.9 3.2 %collective-permute-start.3 = (f32[28,8,128]{2,1,0:T(8,128)S(1)}, f32[28,8,128]{2,1,0:T(8,128)S(1)}, u32[]{:S(2)}, u32[]{:S(2)}) collective-permute-start(f32[28,8,128]{2,1,0:T(8,128)S(1)} %get-tuple-element.31), channel_id=1, source_target_pairs={{0,4},{4,0},{8,12},{12,8},{16,20},{20,16},{24,28},{28,24},{32,36},... | collective-permute-start | bytes 344072 | tf_op jit(solution)/shard_map/ppermute | solution.py:457
  19.1 3.6 %collective-permute-start.4 = (f32[28,8,128]{2,1,0:T(8,128)S(1)}, f32[28,8,128]{2,1,0:T(8,128)S(1)}, u32[]{:S(2)}, u32[]{:S(2)}) collective-permute-start(f32[28,8,128]{2,1,0:T(8,128)S(1)} %get-tuple-element.32), channel_id=1, source_target_pairs={{0,252},{8,4},{16,12},{24,20},{32,28},{40,36},{48,44},{56,52},{64,... | collective-permute-start | bytes 344072 | tf_op jit(solution)/shard_map/ppermute | solution.py:472
  22.7 0.7 %collective-permute-done.2.forth.forth_ref = f32[28,8,128]{2,1,0:T(8,128)S(1)} collective-permute-done((f32[28,8,128]{2,1,0:T(8,128)S(1)}, f32[28,8,128]{2,1,0:T(8,128)S(1)}, u32[]{:S(2)}, u32[]{:S(2)}) %collective-permute-start.2) | collective-permute-done | bytes 114720 | tf_op jit(solution)/shard_map/ppermute | solution.py:458
  23.4 8.2 %late.1 = (f32[2304,128]{1,0:T(8,128)S(1)}, bf16[18,32,128]{2,1,0:T(8,128)(2,1)S(1)}) custom-call(bf16[18,128,256]{2,1,0:T(8,128)(2,1)S(1)} %get-tuple-element.19.own_ref, s32[768,128]{1,0:T(8,128)S(1)} %get-tuple-element.20.off_ref, bf16[384,1024]{1,0:T(8,128)(2,1)S(1)} %get-tuple-element.21.matrix_ref, f32[672,128]{1,0:T(8,128)S(1)} %collective-permute-done.t1_ref, ...), custom_call_target="tpu_custom_call" | custom-call | flops 10000000000 | bytes 1000000 | tf_op jit(solution)/shard_map/late/pallas_call | solution.py:489
  31.6 0.0 collective-permute-done.3.a_ref
  31.6 0.2 early_edges.1.out_in
  31.8 0.0 collective-permute-done.4.back_ref
  31.8 3.2 %late_edges.1 = f32[6,24,16,128]{3,2,1,0:T(8,128)} custom-call(bf16[18,128,256]{2,1,0:T(8,128)(2,1)S(1)} %get-tuple-element.19.own_ref, s32[768,128]{1,0:T(8,128)S(1)} %get-tuple-element.20.off_ref, bf16[384,1024]{1,0:T(8,128)(2,1)S(1)} %get-tuple-element.21.matrix_ref, ...), custom_call_target="tpu_custom_call", output_to_operand_aliasing={{}: (8, {})} | custom-call | tf_op jit(solution)/shard_map/late_edges/pallas_call | solution.py:499
  (2 shorter events, 0.0 us)
Async XLA Ops:
  0.0 5.4 %copy-start.1 = (f32[2,24,16,128]{3,2,1,0:T(8,128)S(1)}, f32[2,24,16,128]{3,2,1,0:T(8,128)}, u32[]{:S(2)}) copy-start(f32[2,24,16,128]{3,2,1,0:T(8,128)} %wind_hbm.1) | copy-start | bytes 1179652
  0.0 5.4 %copy-start = (f32[4,24,16,128]{3,2,1,0:T(8,128)S(1)}, f32[4,24,16,128]{3,2,1,0:T(8,128)}, u32[]{:S(2)}) copy-start(f32[4,24,16,128]{3,2,1,0:T(8,128)} %tracer_hbm.1) | copy-start | bytes 2359300
  2.8 4.3 %collective-permute-start = (f32[672,128]{1,0:T(8,128)}, f32[672,128]{1,0:T(8,128)S(1)}, u32[]{:S(2)}, u32[]{:S(2)}) collective-permute-start(f32[672,128]{1,0:T(8,128)} %get-tuple-element.22), channel_id=1, source_target_pairs={{0,1},{1,0},{2,3},{3,2},{4,5},{5,4},{6,7},{7,6},{8,9},{9,8},{10,11... | collective-permute-start | bytes 1032200 | tf_op jit(solution)/shard_map/ppermute | solution.py:433
  2.9 11.7 %copy-start.2 = (f32[36,8,128]{2,1,0:T(8,128)S(1)}, f32[36,8,128]{2,1,0:T(8,128)}, u32[]{:S(2)}) copy-start(f32[36,8,128]{2,1,0:T(8,128)} %get-tuple-element.24.edges) | copy-start | bytes 442372
  2.9 11.6 %collective-permute-start.1 = (f32[672,128]{1,0:T(8,128)}, f32[672,128]{1,0:T(8,128)S(1)}, u32[]{:S(2)}, u32[]{:S(2)}) collective-permute-start(f32[672,128]{1,0:T(8,128)} %get-tuple-element.23), channel_id=1, source_target_pairs={{1,2},{2,1},{5,6},{6,5},{9,10},{10,9},{13,14},{14,13},{17,18},{18,... | collective-permute-start | bytes 1032200 | tf_op jit(solution)/shard_map/ppermute | solution.py:434
  5.4 1.0 %copy-start.3 = (s32[2,24,16,128]{3,2,1,0:T(8,128)S(1)}, s32[2,24,16,128]{3,2,1,0:T(8,128)}, u32[]{:S(2)}) copy-start(s32[2,24,16,128]{3,2,1,0:T(8,128)} %off_ref.1) | copy-start | bytes 1179652
  14.6 8.8 %collective-permute-start.2 = (f32[28,8,128]{2,1,0:T(8,128)S(1)}, f32[28,8,128]{2,1,0:T(8,128)S(1)}, u32[]{:S(2)}, u32[]{:S(2)}) collective-permute-start(f32[28,8,128]{2,1,0:T(8,128)S(1)} %get-tuple-element.25), channel_id=1, source_target_pairs={{4,8},{12,16},{20,24},{28,32},{36,40},{44,48},{52,56},{60,64},{68,... | collective-permute-start | bytes 344072 | tf_op jit(solution)/shard_map/ppermute | solution.py:458
  15.9 15.7 %collective-permute-start.3 = (f32[28,8,128]{2,1,0:T(8,128)S(1)}, f32[28,8,128]{2,1,0:T(8,128)S(1)}, u32[]{:S(2)}, u32[]{:S(2)}) collective-permute-start(f32[28,8,128]{2,1,0:T(8,128)S(1)} %get-tuple-element.31), channel_id=1, source_target_pairs={{0,4},{4,0},{8,12},{12,8},{16,20},{20,16},{24,28},{28,24},{32,36},... | collective-permute-start | bytes 344072 | tf_op jit(solution)/shard_map/ppermute | solution.py:457
  19.1 12.7 %collective-permute-start.4 = (f32[28,8,128]{2,1,0:T(8,128)S(1)}, f32[28,8,128]{2,1,0:T(8,128)S(1)}, u32[]{:S(2)}, u32[]{:S(2)}) collective-permute-start(f32[28,8,128]{2,1,0:T(8,128)S(1)} %get-tuple-element.32), channel_id=1, source_target_pairs={{0,252},{8,4},{16,12},{24,20},{32,28},{40,36},{48,44},{56,52},{64,... | collective-permute-start | bytes 344072 | tf_op jit(solution)/shard_map/ppermute | solution.py:472

commit v3 on v2

--- a/solution.py
+++ b/solution.py
@@ -19,6 +19,7 @@
 NARROW = 2 * 8 * SIDE
 PAYLOAD = EDGE + 2 * SIDE
 STRIP = 24
+STRIDE = 2 * STRIP + 8
 TALL = COLS + 8
 EARLY = 16
 VMEM_LIMIT = 24 * 1024 * 1024
@@ -68,6 +69,7 @@
         t2_ref[start : start + 8] = pick(lat_even, top, bottom)
 
     put(0, zero, zero)
+    t2_ref[MAIN + NARROW : MAIN + NARROW + 8] = zero
     put(MAIN - 8, zero, zero)
     for field in range(FIELDS):
         copies[field].wait()
@@ -314,14 +316,19 @@
 
 
 def edge_work(
-    own_ref, off_ref, matrix_ref, beside, result, a_ref, forth_ref, back_ref, out_ref, rows, shifted, staged, sems
+    own_ref, off_ref, matrix_ref, beside, result, a_ref, b_refs, out_ref, rows, shifted, staged, sems
 ):
     lon_even = parities()[0]
     slot = lane_slot((8, COLS))
 
+    late = lax.axis_index("lon") % EARLY == EARLY - 1
+
     def sides(place):
-        west = forth_ref[place] if back_ref is None else pick(lon_even, forth_ref[place], a_ref[place])
-        east = a_ref[place] if back_ref is None else pick(lon_even, a_ref[place], back_ref[place])
+        if len(b_refs) == 1:
+            return b_refs[0][place], a_ref[place]
+        swapped = b_refs[0][place]
+        west = pick(lon_even, swapped, a_ref[place])
+        east = pick(lon_even, a_ref[place], pick(late, b_refs[1][place], swapped))
         return west, east
 
     for packed in range(SIDE):
@@ -352,7 +359,7 @@
         for edge in range(EDGE):
             for half in range(2):
                 part = spread[edge * 2 * STRIP : (edge + 1) * 2 * STRIP, half * COLS : (half + 1) * COLS]
-                start = (8 * edge + 2 * pair + half) * 2 * STRIP
+                start = (8 * edge + 2 * pair + half) * STRIDE
                 shifted[start : start + 8] = part[32:40]
                 shifted[start + 8 : start + 40] = part[0:32]
                 shifted[start + 40 : start + 48] = part[40:48]
@@ -363,7 +370,7 @@
         for side in range(2):
             target = (COLS - 8) * side + COLS * group
             other = target + GROUPS * COLS
-            load, here = block_access(shifted, (16 * group + side) * STRIP, 2 * STRIP)
+            load, here = block_access(shifted, 8 * STRIDE * group + STRIP * side, STRIDE)
 
             def emit(field, value):
                 values[field, side] = value
@@ -388,15 +395,15 @@
 def early_edge_kernel(own_ref, off_ref, matrix_ref, beside, result, a_ref, forth_ref, out_ref, *scratch):
     @pl.when(lax.axis_index("lon") % EARLY == 0)
     def _():
-        edge_work(own_ref, off_ref, matrix_ref, beside, result, a_ref, forth_ref, None, out_ref, *scratch)
+        edge_work(own_ref, off_ref, matrix_ref, beside, result, a_ref, (forth_ref,), out_ref, *scratch)
 
 
 def late_edge_kernel(
-    own_ref, off_ref, matrix_ref, beside, result, a_ref, forth_ref, back_ref, out_in, out_ref, *scratch
+    own_ref, off_ref, matrix_ref, beside, result, a_ref, swap_ref, back_ref, out_in, out_ref, *scratch
 ):
     @pl.when(lax.axis_index("lon") % EARLY != 0)
     def _():
-        edge_work(own_ref, off_ref, matrix_ref, beside, result, a_ref, forth_ref, back_ref, out_ref, *scratch)
+        edge_work(own_ref, off_ref, matrix_ref, beside, result, a_ref, (swap_ref, back_ref), out_ref, *scratch)
 
 
 def cost(flops):
@@ -416,7 +423,7 @@
     cells_shape = pltpu.VMEM((FIELDS, LEVS, ROWS, COLS), f32)
     edges, t1, t2 = pl.pallas_call(
         pack_kernel,
-        out_shape=(sds((2 * EDGE, 8, COLS), f32), lat_shape, lat_shape),
+        out_shape=(sds((2 * EDGE, 8, COLS), f32), lat_shape, sds((MAIN + NARROW + 8, COLS), f32)),
         in_specs=[hbm] * 2,
         out_specs=(vmem,) * 3,
         scratch_shapes=[cells_shape, pltpu.SemaphoreType.DMA((FIELDS,))],
@@ -425,8 +432,9 @@
     )(wind, tracers)
     count = lax.axis_size("lon")
     lon_pairs = [(i, i ^ 1) for i in range(count)]
-    lon_forth = [(i, (i + 1) % count) for i in range(1, count, 2)]
-    lon_back = [(i, (i - 1) % count) for i in range(0, count, 2)]
+    lon_forth = [(i, (i + 1) % count) for i in range(EARLY - 1, count, EARLY)]
+    lon_back = [(i, (i - 1) % count) for i in range(0, count, EARLY)]
+    lon_swap = [(i, i + 1 if i % 2 else i - 1) for i in range(count) if 0 < i % EARLY < EARLY - 1]
     lats = lax.axis_size("lat")
     lat_pairs = [(i, i ^ 1) for i in range(lats)]
     lat_middle = [(i, i + 1 if i % 2 else i - 1) for i in range(1, lats - 1)]
@@ -455,6 +463,7 @@
         name="sides",
     )(edges, t1, t2)
     side_a = lax.ppermute(side_a, "lon", lon_pairs)
+    swap = lax.ppermute(forth, "lon", lon_swap)
     forth = lax.ppermute(forth, "lon", lon_forth)
     result_shapes = (sds((EDGE * COLS, COLS), f32), sds((EDGE, 32, COLS), jnp.bfloat16))
     scratch = [pltpu.VMEM((EDGE, COLS, COLS), jnp.bfloat16), pltpu.VMEM((EDGE * 8 * TALL, COLS), f32)]
@@ -472,7 +481,7 @@
     back = lax.ppermute(back, "lon", lon_back)
     edge_scratch = [
         pltpu.VMEM((EDGE, 2 * STRIP, DEPTH), jnp.bfloat16),
-        pltpu.VMEM((EDGE * 8 * 2 * STRIP, COLS), f32),
+        pltpu.VMEM((EDGE * 8 * STRIDE, COLS), f32),
         pltpu.VMEM((GROUPS, FIELDS, 8, ROWS, COLS), f32),
         pltpu.SemaphoreType.DMA((GROUPS, FIELDS)),
     ]
@@ -505,7 +514,7 @@
         input_output_aliases={8: 0},
         compiler_params=params,
         name="late_edges",
-    )(own, turned_off, matrix, beside, result, side_a, forth, back, out)
+    )(own, turned_off, matrix, beside, result, side_a, swap, back, out)
 
 
 def solution(mesh):

time: 35.2 us -> 35.9 us (1.020)
  the two profiles are of different devices: /device:TPU:144 before, /device:TPU:1 now
where the time goes in v3:
time: 35.9 us; the launch traced here: 35.7 us
  Pallas kernels  15.3 us (43%)
  starting transfers between devices  11.1 us (31%)
  waiting for transfers between devices  8.15 us (23%)
  local copies, waits for them, and re-layouts  1 us (3%)
    pallas_call x1, Pallas kernels, shards(): pl.pallas_call(early_kernel, out_shape=result_shapes + (side_shape,), in_...  8.24 us
    ppermute x1, waiting for transfers between devices, shards(): t2 = lax.ppermute(t2, 'lat', lat_middle)  8.13 us
    ppermute x1, starting transfers between devices, shards(): t1 = lax.ppermute(t1, 'lat', lat_pairs)  3.33 us
    pallas_call x1, Pallas kernels, shards(): pl.pallas_call(early_edge_kernel, out_shape=sds((FIELDS, LEVS, ROWS, COLS...  3.22 us
    ppermute x1, starting transfers between devices, shards(): t2 = lax.ppermute(t2, 'lat', lat_middle)  3.12 us
    pallas_call x1, Pallas kernels, shards(): pl.pallas_call(pack_kernel, out_shape=(sds((2 * EDGE, 8, COLS), f32), lat...  2.8 us
    ppermute x1, starting transfers between devices, shards(): back = lax.ppermute(back, 'lon', lon_back)  2.6 us
    ppermute x1, starting transfers between devices, shards(): forth = lax.ppermute(forth, 'lon', lon_forth)  1.29 us
  transfers between devices with their start and end apart: 6, of which 1 were waited for; matrix products, arithmetic and copies ran while one was open for 0% of the time, Pallas kernels for 34%

profile of v3, /device:TPU:1, one launch (start us, length us, event | category | flops | bytes accessed | tf_op | source)
XLA Modules:
  0.0 35.7 jit_solution(8987329058820539743)
XLA Ops:
  0.0 0.0 copy-start.1
  0.0 0.0 copy-start
  0.0 2.8 %pack.1 = (f32[36,8,128]{2,1,0:T(8,128)}, f32[672,128]{1,0:T(8,128)}, f32[680,128]{1,0:T(8,128)}) custom-call(f32[2,24,16,128]{3,2,1,0:T(8,128)} %wind_hbm.1, f32[4,24,16,128]{3,2,1,0:T(8,128)} %tracer_hbm.1), custom_call_target="tpu_custom_call" | custom-call | tf_op jit(solution)/shard_map/pack/pallas_call | solution.py:424
  2.8 3.3 %collective-permute-start = (f32[672,128]{1,0:T(8,128)}, f32[672,128]{1,0:T(8,128)S(1)}, u32[]{:S(2)}, u32[]{:S(2)}) collective-permute-start(f32[672,128]{1,0:T(8,128)} %get-tuple-element.22), channel_id=1, source_target_pairs={{0,1},{1,0},{2,3},{3,2},{4,5},{5,4},{6,7},{7,6},{8,9},{9,8},{10,11... | collective-permute-start | bytes 1032200 | tf_op jit(solution)/shard_map/ppermute | solution.py:441
  6.1 0.0 copy-start.2
  6.1 3.1 %collective-permute-start.1 = (f32[680,128]{1,0:T(8,128)}, f32[680,128]{1,0:T(8,128)S(1)}, u32[]{:S(2)}, u32[]{:S(2)}) collective-permute-start(f32[680,128]{1,0:T(8,128)} %get-tuple-element.23), channel_id=1, source_target_pairs={{1,2},{2,1},{5,6},{6,5},{9,10},{10,9},{13,14},{14,13},{17,18},{18,... | collective-permute-start | bytes 1044488 | tf_op jit(solution)/shard_map/ppermute | solution.py:442
  9.3 0.0 copy-done.1
  9.3 0.0 copy-done
  9.3 0.0 copy-start.3
  9.3 1.0 %copy-done.3 = s32[2,24,16,128]{3,2,1,0:T(8,128)S(1)} copy-done((s32[2,24,16,128]{3,2,1,0:T(8,128)S(1)}, s32[2,24,16,128]{3,2,1,0:T(8,128)}, u32[]{:S(2)}) %copy-start.3) | copy-done | bytes 393240
  10.3 0.7 %own.1 = (bf16[18,128,256]{2,1,0:T(8,128)(2,1)S(1)}, s32[768,128]{1,0:T(8,128)S(1)}, bf16[384,1024]{1,0:T(8,128)(2,1)S(1)}) custom-call(f32[2,24,16,128]{3,2,1,0:T(8,128)S(1)} %copy-done.1, f32[4,24,16,128]{3,2,1,0:T(8,128)S(1)} %copy-done, s32[2,24,16,128]{3,2,1,0:T(8,128)S(1)} %copy-done.3), custom_call_target="tpu_custom_call" | custom-call | flops 20000000000 | bytes 1000000 | tf_op jit(solution)/shard_map/own/pallas_call | solution.py:443
  11.0 0.0 collective-permute-done.t1_ref
  11.0 8.1 %collective-permute-done.1.t2_ref = f32[680,128]{1,0:T(8,128)S(1)} collective-permute-done((f32[680,128]{1,0:T(8,128)}, f32[680,128]{1,0:T(8,128)S(1)}, u32[]{:S(2)}, u32[]{:S(2)}) %collective-permute-start.1) | collective-permute-done | bytes 348192 | tf_op jit(solution)/shard_map/ppermute | solution.py:442
  19.2 0.0 copy-done.2
  19.2 1.3 %collective-permute-start.2 = (f32[28,8,128]{2,1,0:T(8,128)S(1)}, f32[28,8,128]{2,1,0:T(8,128)S(1)}, u32[]{:S(2)}, u32[]{:S(2)}) collective-permute-start(f32[28,8,128]{2,1,0:T(8,128)S(1)} %get-tuple-element.25), channel_id=1, source_target_pairs={{60,64},{124,128},{188,192},{252,0},{61,65},{125,129},{189,193},{2... | collective-permute-start | bytes 344072 | tf_op jit(solution)/shard_map/ppermute | solution.py:467
  20.5 0.7 %collective-permute-start.4 = (f32[28,8,128]{2,1,0:T(8,128)S(1)}, f32[28,8,128]{2,1,0:T(8,128)S(1)}, u32[]{:S(2)}, u32[]{:S(2)}) collective-permute-start(f32[28,8,128]{2,1,0:T(8,128)S(1)} %get-tuple-element.25), channel_id=1, source_target_pairs={{4,8},{8,4},{12,16},{16,12},{20,24},{24,20},{28,32},{32,28},{36,40... | collective-permute-start | bytes 344072 | tf_op jit(solution)/shard_map/ppermute | solution.py:466
  21.2 0.1 collective-permute-start.3
  21.3 8.2 %early.1 = (f32[2304,128]{1,0:T(8,128)S(1)}, bf16[18,32,128]{2,1,0:T(8,128)(2,1)S(1)}, f32[28,8,128]{2,1,0:T(8,128)S(1)}) custom-call(bf16[18,128,256]{2,1,0:T(8,128)(2,1)S(1)} %get-tuple-element.19.own_ref, s32[768,128]{1,0:T(8,128)S(1)} %get-tuple-element.20.off_ref, ...), custom_call_target="tpu_custom_call", output_to_operand_aliasing={{2}: (5, {})} | custom-call | flops 10000000000 | bytes 1000000 | tf_op jit(solution)/shard_map/early/pallas_call | solution.py:470
  29.6 2.6 %collective-permute-start.5 = (f32[28,8,128]{2,1,0:T(8,128)S(1)}, f32[28,8,128]{2,1,0:T(8,128)S(1)}, u32[]{:S(2)}, u32[]{:S(2)}) collective-permute-start(f32[28,8,128]{2,1,0:T(8,128)S(1)} %get-tuple-element.32), channel_id=1, source_target_pairs={{0,252},{64,60},{128,124},{192,188},{1,253},{65,61},{129,125},{193... | collective-permute-start | bytes 344072 | tf_op jit(solution)/shard_map/ppermute | solution.py:481
  32.2 0.0 collective-permute-done.2.forth.forth_ref
  32.2 0.1 late.1
  32.3 0.0 collective-permute-done.3.a_ref
  32.3 3.2 %early_edges.1.out_in = f32[6,24,16,128]{3,2,1,0:T(8,128)} custom-call(bf16[18,128,256]{2,1,0:T(8,128)(2,1)S(1)} %get-tuple-element.19.own_ref, s32[768,128]{1,0:T(8,128)S(1)} %get-tuple-element.20.off_ref, bf16[384,1024]{1,0:T(8,128)(2,1)S(1)} %get-tuple-element.21.matrix_ref, bf16[18,32,128]{2,1,0:T(8,128)(2,1)S(1)} %get-tuple-element.28.beside_in.beside, ...), custom_call_target="tpu_custom_call" | custom-call | flops 10000000000 | bytes 1000000 | tf_op jit(solution)/shard_map/early_edges/pallas_call | solution.py:488
  35.5 0.0 collective-permute-done.4.swap_ref
  35.5 0.0 collective-permute-done.5.back_ref
  35.5 0.2 late_edges.1
  (1 shorter events, 0.0 us)
Async XLA Ops:
  0.0 9.3 %copy-start.1 = (f32[2,24,16,128]{3,2,1,0:T(8,128)S(1)}, f32[2,24,16,128]{3,2,1,0:T(8,128)}, u32[]{:S(2)}) copy-start(f32[2,24,16,128]{3,2,1,0:T(8,128)} %wind_hbm.1) | copy-start | bytes 1179652
  0.0 9.3 %copy-start = (f32[4,24,16,128]{3,2,1,0:T(8,128)S(1)}, f32[4,24,16,128]{3,2,1,0:T(8,128)}, u32[]{:S(2)}) copy-start(f32[4,24,16,128]{3,2,1,0:T(8,128)} %tracer_hbm.1) | copy-start | bytes 2359300
  2.8 8.2 %collective-permute-start = (f32[672,128]{1,0:T(8,128)}, f32[672,128]{1,0:T(8,128)S(1)}, u32[]{:S(2)}, u32[]{:S(2)}) collective-permute-start(f32[672,128]{1,0:T(8,128)} %get-tuple-element.22), channel_id=1, source_target_pairs={{0,1},{1,0},{2,3},{3,2},{4,5},{5,4},{6,7},{7,6},{8,9},{9,8},{10,11... | collective-permute-start | bytes 1032200 | tf_op jit(solution)/shard_map/ppermute | solution.py:441
  6.1 13.0 %copy-start.2 = (f32[36,8,128]{2,1,0:T(8,128)S(1)}, f32[36,8,128]{2,1,0:T(8,128)}, u32[]{:S(2)}) copy-start(f32[36,8,128]{2,1,0:T(8,128)} %get-tuple-element.24.edges) | copy-start | bytes 442372
  6.1 13.0 %collective-permute-start.1 = (f32[680,128]{1,0:T(8,128)}, f32[680,128]{1,0:T(8,128)S(1)}, u32[]{:S(2)}, u32[]{:S(2)}) collective-permute-start(f32[680,128]{1,0:T(8,128)} %get-tuple-element.23), channel_id=1, source_target_pairs={{1,2},{2,1},{5,6},{6,5},{9,10},{10,9},{13,14},{14,13},{17,18},{18,... | collective-permute-start | bytes 1044488 | tf_op jit(solution)/shard_map/ppermute | solution.py:442
  9.3 1.0 %copy-start.3 = (s32[2,24,16,128]{3,2,1,0:T(8,128)S(1)}, s32[2,24,16,128]{3,2,1,0:T(8,128)}, u32[]{:S(2)}) copy-start(s32[2,24,16,128]{3,2,1,0:T(8,128)} %off_ref.1) | copy-start | bytes 1179652
  19.2 13.0 %collective-permute-start.2 = (f32[28,8,128]{2,1,0:T(8,128)S(1)}, f32[28,8,128]{2,1,0:T(8,128)S(1)}, u32[]{:S(2)}, u32[]{:S(2)}) collective-permute-start(f32[28,8,128]{2,1,0:T(8,128)S(1)} %get-tuple-element.25), channel_id=1, source_target_pairs={{60,64},{124,128},{188,192},{252,0},{61,65},{125,129},{189,193},{2... | collective-permute-start | bytes 344072 | tf_op jit(solution)/shard_map/ppermute | solution.py:467
  20.5 15.0 %collective-permute-start.4 = (f32[28,8,128]{2,1,0:T(8,128)S(1)}, f32[28,8,128]{2,1,0:T(8,128)S(1)}, u32[]{:S(2)}, u32[]{:S(2)}) collective-permute-start(f32[28,8,128]{2,1,0:T(8,128)S(1)} %get-tuple-element.25), channel_id=1, source_target_pairs={{4,8},{8,4},{12,16},{16,12},{20,24},{24,20},{28,32},{32,28},{36,40... | collective-permute-start | bytes 344072 | tf_op jit(solution)/shard_map/ppermute | solution.py:466
  21.2 11.1 %collective-permute-start.3 = (f32[28,8,128]{2,1,0:T(8,128)S(1)}, f32[28,8,128]{2,1,0:T(8,128)S(1)}, u32[]{:S(2)}, u32[]{:S(2)}) collective-permute-start(f32[28,8,128]{2,1,0:T(8,128)S(1)} %get-tuple-element.31), channel_id=1, source_target_pairs={{0,4},{4,0},{8,12},{12,8},{16,20},{20,16},{24,28},{28,24},{32,36},... | collective-permute-start | bytes 344072 | tf_op jit(solution)/shard_map/ppermute | solution.py:465
  29.6 6.0 %collective-permute-start.5 = (f32[28,8,128]{2,1,0:T(8,128)S(1)}, f32[28,8,128]{2,1,0:T(8,128)S(1)}, u32[]{:S(2)}, u32[]{:S(2)}) collective-permute-start(f32[28,8,128]{2,1,0:T(8,128)S(1)} %get-tuple-element.32), channel_id=1, source_target_pairs={{0,252},{64,60},{128,124},{192,188},{1,253},{65,61},{129,125},{193... | collective-permute-start | bytes 344072 | tf_op jit(solution)/shard_map/ppermute | solution.py:481
